TPU v7x, 256 devices: a whole 4x4x8 slice. The times are simulated.
256 devices in a mesh: cfg: 2 (over x_hi), blk: 16 (over z, core), uly: 8 (over x_lo, y).
Axes of the slice: x: 4 (x_hi: 2, x_lo: 2; x = x_hi * 2 + x_lo), y: 4, z: 8, core: 2. Of those that a mesh axis runs over, the one named last changes fastest.
Arguments:
- queries: bfloat16 [32768, 3072], P(('cfg', 'blk', 'uly')), parts along dimension 0, may hold values from -6 to 6
- key_states: bfloat16 [32768, 3072], P(('cfg', 'blk', 'uly')), parts along dimension 0, may hold values from -6 to 6
- value_states: bfloat16 [32768, 3072], P(('cfg', 'blk', 'uly')), parts along dimension 0, may hold values from -6 to 6
- query_gain: float32 [128], replicated, may hold values from 0.1 to 1.9
- key_gain: float32 [128], replicated, may hold values from 0.1 to 1.9
- neighbors: int32 [256, 27], P('blk'), may hold values from 0 to 255, as said below
- counts: int32 [256], P('blk'), may hold values from 1 to 27, as said below
Outputs:
- attended: bfloat16 [32768, 3072], P(('cfg', 'blk', 'uly')), parts along dimension 0
There are 2 independent parts, one for each index of `cfg`. A program takes and returns all parts, laid end to end along the dimension named above; an argument that names none is the same for every part. Nothing has to cross between parts.
Inputs may be any that keep to these rules, and one draw needn't show every extreme that they name: `neighbors`: tiles are numbered frame by frame on a grid of 3 x 20 tiles a frame (number = frame 3 * 20 + row 20 + column; the last frame may be partial). The first counts[i] entries of row i are distinct tiles of the 3 x 3 x 3 block of tiles around tile i, tile i among them; the other entries equal i. Every entry differs from i by at most 81, and that distance is reached. `counts`: number of live entries at the head of each row of neighbors.
All inputs are finite; a program needn't handle non-finite values.
Results may differ from a plain program's by a relative error of at most 0.0078.
Values may be sent and summed in bfloat16 or wider, within the bound.
A program may use at most 128 MiB of HBM per device.

v0:
```python
import math

import jax
import jax.numpy as jnp
from jax import lax
from jax.sharding import PartitionSpec as P

MAXOFF = 81


def from_behind(value, axis, steps):
    count = lax.axis_size(axis)
    initial, last = (max(0, -steps), min(count, count - steps))
    return lax.ppermute(value, axis, [(source, source + steps) for source in range(initial, last)])


def normalize(states, gain):
    widened = states.astype(jnp.float32)
    factor = lax.rsqrt(jnp.mean(widened * widened, axis=-1, keepdims=True) + 1e-06)
    return (widened * factor * gain).astype(jnp.bfloat16)


def attend_group(query_tiles, key_tiles, value_tiles, neighbor_rows, count_rows):
    near_keys = key_tiles[neighbor_rows]
    near_values = value_tiles[neighbor_rows]
    factor = query_tiles.shape[-1] ** (-0.5)
    scores = (
        jnp.einsum("bihe,bnjhe->bhinj", query_tiles, near_keys, preferred_element_type=jnp.float32)
        * factor
    )
    slot_ids = jnp.arange(neighbor_rows.shape[1], dtype=jnp.int32)
    live_slot = slot_ids[None, :] < count_rows[:, None]
    weights = jnp.where(live_slot[:, None, None, :, None], jnp.exp(scores), jnp.float32(0.0))
    totals = jnp.sum(weights, axis=(3, 4), keepdims=True)
    shares = (weights / totals).astype(jnp.bfloat16)
    mixed = jnp.einsum("bhinj,bnjhe->bihe", shares, near_values, preferred_element_type=jnp.float32)
    return mixed.astype(jnp.bfloat16)


def per_device(queries, key_states, value_states, query_gain, key_gain, neighbors, counts):
    tokens, width = queries.shape
    head_dim = query_gain.shape[0]
    heads = width // head_dim
    blocks = lax.axis_size("blk")

    def split_heads(states):
        return states.reshape(tokens, heads, head_dim)

    q_heads, k_heads, v_heads = (
        lax.all_to_all(split_heads(queries), "uly", split_axis=1, concat_axis=0, tiled=True),
        lax.all_to_all(split_heads(key_states), "uly", split_axis=1, concat_axis=0, tiled=True),
        lax.all_to_all(split_heads(value_states), "uly", split_axis=1, concat_axis=0, tiled=True),
    )
    local_heads = k_heads.shape[1]
    stacked = jnp.stack((normalize(k_heads, key_gain), v_heads))
    length = stacked.shape[1]
    shard_tiles = length // 64
    reach = min(-(-MAXOFF // shard_tiles), blocks - 1)
    lower_pieces = []
    upper_pieces = []
    for offset in range(reach, 0, -1):
        lower_pieces.append(from_behind(stacked, "blk", offset))
    for offset in range(1, reach + 1):
        upper_pieces.append(from_behind(stacked, "blk", -offset))
    before = reach * shard_tiles
    gathered = jnp.concatenate(lower_pieces + [stacked] + upper_pieces, axis=1)
    key_tiles = gathered[0].reshape(-1, 64, local_heads, head_dim)
    value_tiles = gathered[1].reshape(-1, 64, local_heads, head_dim)
    base_tile = lax.axis_index("blk") * shard_tiles - before
    local_rows = neighbors - base_tile
    query_tiles = normalize(q_heads, query_gain).reshape(shard_tiles, 64, local_heads, head_dim)
    group = math.gcd(shard_tiles, 4)
    slots = neighbors.shape[1]

    def one_group(items):
        return attend_group(items[0], key_tiles, value_tiles, items[1], items[2])

    result = lax.map(
        one_group,
        (
            query_tiles.reshape(shard_tiles // group, group, 64, local_heads, head_dim),
            local_rows.reshape(shard_tiles // group, group, slots),
            counts.reshape(shard_tiles // group, group),
        ),
    )
    mixed = result.reshape(length, local_heads, head_dim)
    returned = lax.all_to_all(mixed, "uly", split_axis=0, concat_axis=1, tiled=True)
    return returned.reshape(tokens, width)


def solution(mesh):
    return jax.shard_map(
        per_device,
        mesh=mesh,
        in_specs=(
            P(("cfg", "blk", "uly"), None),
            P(("cfg", "blk", "uly"), None),
            P(("cfg", "blk", "uly"), None),
            P(),
            P(),
            P("blk", None),
            P("blk"),
        ),
        out_specs=P(("cfg", "blk", "uly"), None),
        check_vma=False,
    )
```

profile of v0, /device:TPU:64, one launch (start us, length us, event | category | flops | bytes accessed | tf_op | source)
XLA Modules:
  0.0 926.7 jit_solution(3480835358334464228)
XLA Ops:
  0.0 2.3 copy.44
  2.3 5.4 all-to-all-start
  7.7 2.3 copy.47
  10.0 9.7 %all-to-all-done = bf16[128,24,128]{0,2,1:T(8,128)(2,1)S(1)} async-done(((bf16[128,24,128]{0,2,1:T(8,128)(2,1)}), bf16[128,24,128]{0,2,1:T(8,128)(2,1)S(1)}, u32[]{:S(2)}, u32[]{:S(2)}) %all-to-all-start) | async-done | bytes 786464 | tf_op jit(solution)/shard_map/all_to_all | solution.py:51
  19.7 3.6 all-to-all-start.1
  25.4 10.1 %all-to-all-done.1 = bf16[128,24,128]{0,2,1:T(8,128)(2,1)S(1)} async-done(((bf16[128,24,128]{0,2,1:T(8,128)(2,1)}), bf16[128,24,128]{0,2,1:T(8,128)(2,1)S(1)}, u32[]{:S(2)}, u32[]{:S(2)}) %all-to-all-start.1) | async-done | bytes 786464 | tf_op jit(solution)/shard_map/all_to_all | solution.py:52
  39.1 8.0 collective-permute-start
  47.1 2.4 collective-permute-start.1
  49.5 1.9 collective-permute-start.2
  51.4 1.9 collective-permute-start.3
  53.4 1.9 collective-permute-start.4
  55.3 73.5 %collective-permute-done = bf16[2,1024,3,128]{3,1,2,0:T(8,128)(2,1)} collective-permute-done((bf16[2,1024,3,128]{3,1,2,0:T(8,128)(2,1)}, bf16[2,1024,3,128]{3,1,2,0:T(8,128)(2,1)}, u32[]{:S(2)}, u32[]{:S(2)}) %collective-permute-start) | collective-permute-done | bytes 1572896 | tf_op jit(solution)/shard_map/ppermute | solution.py:14
  128.8 1.9 collective-permute-start.5
  130.7 46.5 %collective-permute-done.1 = bf16[2,1024,3,128]{3,1,2,0:T(8,128)(2,1)} collective-permute-done((bf16[2,1024,3,128]{3,1,2,0:T(8,128)(2,1)}, bf16[2,1024,3,128]{3,1,2,0:T(8,128)(2,1)}, u32[]{:S(2)}, u32[]{:S(2)}) %collective-permute-start.1) | collective-permute-done | bytes 1572896 | tf_op jit(solution)/shard_map/ppermute | solution.py:14
  177.3 54.6 %collective-permute-start.6 = (bf16[2,1024,3,128]{3,1,2,0:T(8,128)(2,1)}, bf16[2,1024,3,128]{3,1,2,0:T(8,128)(2,1)}, u32[]{:S(2)}, u32[]{:S(2)}) collective-permute-start(bf16[2,1024,3,128]{3,1,2,0:T(8,128)(2,1)} %pad_maximum_fusion), channel_id=1, source_target_pairs={{8,0},{16,8},{24,16},{32,24},{40,32},{48,40},{56,48},{64,56},{72,6... | collective-permute-start | bytes 4718600 | tf_op jit(solution)/shard_map/ppermute | solution.py:14
  233.1 4.5 all-to-all-start.2
  237.6 9.4 %all-to-all-done.2 = bf16[128,24,128]{0,2,1:T(8,128)(2,1)S(1)} async-done(((bf16[128,24,128]{0,2,1:T(8,128)(2,1)}), bf16[128,24,128]{0,2,1:T(8,128)(2,1)S(1)}, u32[]{:S(2)}, u32[]{:S(2)}) %all-to-all-start.2) | async-done | bytes 786464 | tf_op jit(solution)/shard_map/all_to_all | solution.py:50
  247.2 67.0 %collective-permute-done.2 = bf16[2,1024,3,128]{3,1,2,0:T(8,128)(2,1)} collective-permute-done((bf16[2,1024,3,128]{3,1,2,0:T(8,128)(2,1)}, bf16[2,1024,3,128]{3,1,2,0:T(8,128)(2,1)}, u32[]{:S(2)}, u32[]{:S(2)}) %collective-permute-start.2) | collective-permute-done | bytes 1572896 | tf_op jit(solution)/shard_map/ppermute | solution.py:14
  314.2 1.9 collective-permute-start.7
  317.4 3.0 copy.52
  320.6 27.3 %collective-permute-done.3 = bf16[2,1024,3,128]{3,1,2,0:T(8,128)(2,1)} collective-permute-done((bf16[2,1024,3,128]{3,1,2,0:T(8,128)(2,1)}, bf16[2,1024,3,128]{3,1,2,0:T(8,128)(2,1)}, u32[]{:S(2)}, u32[]{:S(2)}) %collective-permute-start.3) | collective-permute-done | bytes 1572896 | tf_op jit(solution)/shard_map/ppermute | solution.py:14
  347.9 1.9 collective-permute-start.8
  349.8 31.8 %collective-permute-done.4 = bf16[2,1024,3,128]{3,1,2,0:T(8,128)(2,1)} collective-permute-done((bf16[2,1024,3,128]{3,1,2,0:T(8,128)(2,1)}, bf16[2,1024,3,128]{3,1,2,0:T(8,128)(2,1)}, u32[]{:S(2)}, u32[]{:S(2)}) %collective-permute-start.4) | collective-permute-done | bytes 1572896 | tf_op jit(solution)/shard_map/ppermute | solution.py:14
  386.7 2.9 constant_dynamic-update-slice_fusion.12
  390.9 2.8 constant_dynamic-update-slice_fusion.11
  393.7 2.9 constant_dynamic-update-slice_fusion.10
  396.5 2.9 constant_dynamic-update-slice_fusion.9
  399.4 2.9 constant_dynamic-update-slice_fusion.8
  402.3 2.9 constant_dynamic-update-slice_fusion.7
  406.7 2.9 constant_dynamic-update-slice_fusion.5
  409.6 2.8 constant_dynamic-update-slice_fusion.4
  412.4 22.3 %collective-permute-done.8 = bf16[2,1024,3,128]{3,1,2,0:T(8,128)(2,1)S(1)} collective-permute-done((bf16[2,1024,3,128]{3,1,2,0:T(8,128)(2,1)}, bf16[2,1024,3,128]{3,1,2,0:T(8,128)(2,1)S(1)}, u32[]{:S(2)}, u32[]{:S(2)}) %collective-permute-start.8) | collective-permute-done | bytes 1572896 | tf_op jit(solution)/shard_map/ppermute | solution.py:14
  436.1 45.7 %collective-permute-done.9 = bf16[2,1024,3,128]{3,1,2,0:T(8,128)(2,1)S(1)} collective-permute-done((bf16[2,1024,3,128]{3,1,2,0:T(8,128)(2,1)}, bf16[2,1024,3,128]{3,1,2,0:T(8,128)(2,1)S(1)}, u32[]{:S(2)}, u32[]{:S(2)}) %collective-permute-start.9) | collective-permute-done | bytes 1572896 | tf_op jit(solution)/shard_map/ppermute | solution.py:14
  483.2 41.9 %collective-permute-done.10 = bf16[2,1024,3,128]{3,1,2,0:T(8,128)(2,1)S(1)} collective-permute-done((bf16[2,1024,3,128]{3,1,2,0:T(8,128)(2,1)}, bf16[2,1024,3,128]{3,1,2,0:T(8,128)(2,1)S(1)}, u32[]{:S(2)}, u32[]{:S(2)}) %collective-permute-start.10) | collective-permute-done | bytes 1572896 | tf_op jit(solution)/shard_map/ppermute | solution.py:14
  526.6 133.6 %collective-permute-done.11 = bf16[2,1024,3,128]{3,1,2,0:T(8,128)(2,1)S(1)} collective-permute-done((bf16[2,1024,3,128]{3,1,2,0:T(8,128)(2,1)}, bf16[2,1024,3,128]{3,1,2,0:T(8,128)(2,1)S(1)}, u32[]{:S(2)}, u32[]{:S(2)}) %collective-permute-start.11) | collective-permute-done | bytes 1572896 | tf_op jit(solution)/shard_map/ppermute | solution.py:14
  661.7 7.8 fusion.19
  669.5 13.9 %copy.54 = bf16[208,64,3,128]{3,2,1,0:T(4,128)(2,1)} copy(bf16[208,64,3,128]{3,1,0,2:T(8,128)(2,1)S(1)} %bitcast.91) | data formatting | bytes 20447232 | tf_op jit(solution)/shard_map/while | solution.py:78
  683.4 13.7 %copy.56 = bf16[208,64,3,128]{3,2,1,0:T(4,128)(2,1)} copy(bf16[208,64,3,128]{3,1,0,2:T(8,128)(2,1)S(1)} %bitcast.90) | data formatting | bytes 20447232 | tf_op jit(solution)/shard_map/while | solution.py:78
  697.1 207.6 %while.10 = (s32[]{:T(128)}, bf16[4,4,64,3,128]{4,2,1,0,3:T(8,128)(2,1)S(1)}, s32[4,4,27]{2,1,0:T(4,128)S(1)}, bf16[208,64,3,128]{3,2,1,0:T(4,128)(2,1)}, s32[4,...) while((s32[]{:T(128)}, ...), condition=%wide.region_4.5_spmd, body=%wide.region_2.4_spmd.sunk | while | flops 688865920 | bytes 85734856 | solution.py:78
  697.2 15.1 %gather_fusion = bf16[108,64,3,128]{3,2,1,0:T(4,128)(2,1)} fusion(bf16[208,64,3,128]{3,2,1,0:T(4,128)(2,1)} %get-tuple-element.145, s32[1024]{0:T(1024)S(1)} %pad_clamp_fusion.2), kind=kCustom, calls=%fused_computation.1.clone.1 | custom fusion | bytes 10617264 | tf_op jit(solution)/shard_map/while/body/eval_jaxpr/gather | solution.py:24
  712.3 4.5 copy.88
  718.4 3.9 copy-done
  722.4 2.4 fusion.31
  724.8 15.1 %gather_fusion.1 = bf16[108,64,3,128]{3,2,1,0:T(4,128)(2,1)} fusion(bf16[208,64,3,128]{3,2,1,0:T(4,128)(2,1)} %get-tuple-element.142, s32[1024]{0:T(1024)S(1)} %pad_clamp_fusion.2), kind=kCustom, calls=%fused_computation.clone.1 | custom fusion | bytes 10617264 | tf_op jit(solution)/shard_map/while/body/eval_jaxpr/gather | solution.py:25
  739.9 9.0 fusion.32
  749.1 15.1 %gather_fusion = bf16[108,64,3,128]{3,2,1,0:T(4,128)(2,1)} fusion(bf16[208,64,3,128]{3,2,1,0:T(4,128)(2,1)} %get-tuple-element.145, s32[1024]{0:T(1024)S(1)} %pad_clamp_fusion.2), kind=kCustom, calls=%fused_computation.1.clone.1 | custom fusion | bytes 10617264 | tf_op jit(solution)/shard_map/while/body/eval_jaxpr/gather | solution.py:24
  764.2 4.5 copy.88
  770.4 3.9 copy-done
  774.3 2.4 fusion.31
  776.7 15.1 %gather_fusion.1 = bf16[108,64,3,128]{3,2,1,0:T(4,128)(2,1)} fusion(bf16[208,64,3,128]{3,2,1,0:T(4,128)(2,1)} %get-tuple-element.142, s32[1024]{0:T(1024)S(1)} %pad_clamp_fusion.2), kind=kCustom, calls=%fused_computation.clone.1 | custom fusion | bytes 10617264 | tf_op jit(solution)/shard_map/while/body/eval_jaxpr/gather | solution.py:25
  791.8 9.0 fusion.32
  801.0 15.1 %gather_fusion = bf16[108,64,3,128]{3,2,1,0:T(4,128)(2,1)} fusion(bf16[208,64,3,128]{3,2,1,0:T(4,128)(2,1)} %get-tuple-element.145, s32[1024]{0:T(1024)S(1)} %pad_clamp_fusion.2), kind=kCustom, calls=%fused_computation.1.clone.1 | custom fusion | bytes 10617264 | tf_op jit(solution)/shard_map/while/body/eval_jaxpr/gather | solution.py:24
  816.1 4.5 copy.88
  822.3 3.9 copy-done
  826.2 2.4 fusion.31
  828.6 15.1 %gather_fusion.1 = bf16[108,64,3,128]{3,2,1,0:T(4,128)(2,1)} fusion(bf16[208,64,3,128]{3,2,1,0:T(4,128)(2,1)} %get-tuple-element.142, s32[1024]{0:T(1024)S(1)} %pad_clamp_fusion.2), kind=kCustom, calls=%fused_computation.clone.1 | custom fusion | bytes 10617264 | tf_op jit(solution)/shard_map/while/body/eval_jaxpr/gather | solution.py:25
  843.7 9.0 fusion.32
  852.9 15.1 %gather_fusion = bf16[108,64,3,128]{3,2,1,0:T(4,128)(2,1)} fusion(bf16[208,64,3,128]{3,2,1,0:T(4,128)(2,1)} %get-tuple-element.145, s32[1024]{0:T(1024)S(1)} %pad_clamp_fusion.2), kind=kCustom, calls=%fused_computation.1.clone.1 | custom fusion | bytes 10617264 | tf_op jit(solution)/shard_map/while/body/eval_jaxpr/gather | solution.py:24
  868.0 4.5 copy.88
  874.2 3.9 copy-done
  878.1 2.4 fusion.31
  880.5 15.1 %gather_fusion.1 = bf16[108,64,3,128]{3,2,1,0:T(4,128)(2,1)} fusion(bf16[208,64,3,128]{3,2,1,0:T(4,128)(2,1)} %get-tuple-element.142, s32[1024]{0:T(1024)S(1)} %pad_clamp_fusion.2), kind=kCustom, calls=%fused_computation.clone.1 | custom fusion | bytes 10617264 | tf_op jit(solution)/shard_map/while/body/eval_jaxpr/gather | solution.py:25
  895.6 9.0 fusion.32
  905.4 19.6 %all_to_all.48 = bf16[1024,3,128]{2,1,0:T(4,128)(2,1)S(1)} all-to-all(bf16[1024,3,128]{2,1,0:T(4,128)(2,1)S(1)} %copy.58), channel_id=1, replica_groups=mesh['cfg'=2,'blk'=16,'uly'=8] {'uly'}, dimensions={0} | all-to-all | bytes 1572864 | tf_op jit(solution)/shard_map/all_to_all | solution.py:87
  (76 shorter events, 31.4 us)
Async XLA Ops:
  0.0 35.9 %copy-start.4 = (f32[128]{0:T(128)S(1)}, f32[128]{0:T(128)}, u32[]{:S(2)}) copy-start(f32[128]{0:T(128)} %param.13) | copy-start | bytes 1540
  2.3 17.4 %all-to-all-start = ((bf16[128,24,128]{0,2,1:T(8,128)(2,1)}), bf16[128,24,128]{0,2,1:T(8,128)(2,1)S(1)}, u32[]{:S(2)}, u32[]{:S(2)}) async-start(bf16[128,24,128]{0,2,1:T(8,128)(2,1)} %bitcast.13), calls=%async_computation | async-start | bytes 1572864 | tf_op jit(solution)/shard_map/all_to_all | solution.py:51
  19.7 15.8 %all-to-all-start.1 = ((bf16[128,24,128]{0,2,1:T(8,128)(2,1)}), bf16[128,24,128]{0,2,1:T(8,128)(2,1)S(1)}, u32[]{:S(2)}, u32[]{:S(2)}) async-start(bf16[128,24,128]{0,2,1:T(8,128)(2,1)} %bitcast.20), calls=%async_computation.1 | async-start | bytes 1572864 | tf_op jit(solution)/shard_map/all_to_all | solution.py:52
  23.5 214.0 %copy-start.3 = (s32[16]{0:T(128)S(1)}, s32[16]{0:T(128)}, u32[]{:S(2)}) copy-start(s32[16]{0:T(128)} %param.15) | copy-start | bytes 196
  23.5 214.1 %copy-start.2 = (s32[16,27]{1,0:T(8,128)S(1)}, s32[16,27]{1,0:T(8,128)}, u32[]{:S(2)}) copy-start(s32[16,27]{1,0:T(8,128)} %param.14) | copy-start | bytes 5188
  25.4 206.5 %copy-start.1 = (bf16[128,3072]{1,0:T(8,128)(2,1)S(1)}, bf16[128,3072]{1,0:T(8,128)(2,1)}, u32[]{:S(2)}) copy-start(bf16[128,3072]{1,0:T(8,128)(2,1)} %param.9) | copy-start | bytes 2359300
  35.9 347.6 %copy-start.5 = (f32[128]{0:T(128)S(1)}, f32[128]{0:T(128)}, u32[]{:S(2)}) copy-start(f32[128]{0:T(128)} %param.12) | copy-start | bytes 1540
  39.1 89.7 %collective-permute-start = (bf16[2,1024,3,128]{3,1,2,0:T(8,128)(2,1)}, bf16[2,1024,3,128]{3,1,2,0:T(8,128)(2,1)}, u32[]{:S(2)}, u32[]{:S(2)}) collective-permute-start(bf16[2,1024,3,128]{3,1,2,0:T(8,128)(2,1)} %pad_maximum_fusion), channel_id=1, source_target_pairs={{0,48},{8,56},{16,64},{24,72},{32,80},{40,88},{48,96},{56,104},{64... | collective-permute-start | bytes 4718600 | tf_op jit(solution)/shard_map/ppermute | solution.py:14
  47.1 130.2 %collective-permute-start.1 = (bf16[2,1024,3,128]{3,1,2,0:T(8,128)(2,1)}, bf16[2,1024,3,128]{3,1,2,0:T(8,128)(2,1)}, u32[]{:S(2)}, u32[]{:S(2)}) collective-permute-start(bf16[2,1024,3,128]{3,1,2,0:T(8,128)(2,1)} %pad_maximum_fusion), channel_id=1, source_target_pairs={{0,40},{8,48},{16,56},{24,64},{32,72},{40,80},{48,88},{56,96},{64,... | collective-permute-start | bytes 4718600 | tf_op jit(solution)/shard_map/ppermute | solution.py:14
  49.5 264.6 %collective-permute-start.2 = (bf16[2,1024,3,128]{3,1,2,0:T(8,128)(2,1)}, bf16[2,1024,3,128]{3,1,2,0:T(8,128)(2,1)}, u32[]{:S(2)}, u32[]{:S(2)}) collective-permute-start(bf16[2,1024,3,128]{3,1,2,0:T(8,128)(2,1)} %pad_maximum_fusion), channel_id=1, source_target_pairs={{0,32},{8,40},{16,48},{24,56},{32,64},{40,72},{48,80},{56,88},{64,... | collective-permute-start | bytes 4718600 | tf_op jit(solution)/shard_map/ppermute | solution.py:14
  51.4 296.4 %collective-permute-start.3 = (bf16[2,1024,3,128]{3,1,2,0:T(8,128)(2,1)}, bf16[2,1024,3,128]{3,1,2,0:T(8,128)(2,1)}, u32[]{:S(2)}, u32[]{:S(2)}) collective-permute-start(bf16[2,1024,3,128]{3,1,2,0:T(8,128)(2,1)} %pad_maximum_fusion), channel_id=1, source_target_pairs={{0,24},{8,32},{16,40},{24,48},{32,56},{40,64},{48,72},{56,80},{64,... | collective-permute-start | bytes 4718600 | tf_op jit(solution)/shard_map/ppermute | solution.py:14
  53.4 328.2 %collective-permute-start.4 = (bf16[2,1024,3,128]{3,1,2,0:T(8,128)(2,1)}, bf16[2,1024,3,128]{3,1,2,0:T(8,128)(2,1)}, u32[]{:S(2)}, u32[]{:S(2)}) collective-permute-start(bf16[2,1024,3,128]{3,1,2,0:T(8,128)(2,1)} %pad_maximum_fusion), channel_id=1, source_target_pairs={{0,16},{8,24},{16,32},{24,40},{32,48},{40,56},{48,64},{56,72},{64,... | collective-permute-start | bytes 4718600 | tf_op jit(solution)/shard_map/ppermute | solution.py:14
  128.8 256.6 %collective-permute-start.5 = (bf16[2,1024,3,128]{3,1,2,0:T(8,128)(2,1)}, bf16[2,1024,3,128]{3,1,2,0:T(8,128)(2,1)}, u32[]{:S(2)}, u32[]{:S(2)}) collective-permute-start(bf16[2,1024,3,128]{3,1,2,0:T(8,128)(2,1)} %pad_maximum_fusion), channel_id=1, source_target_pairs={{0,8},{8,16},{16,24},{24,32},{32,40},{40,48},{48,56},{56,64},{64,7... | collective-permute-start | bytes 4718600 | tf_op jit(solution)/shard_map/ppermute | solution.py:14
  177.3 212.3 %collective-permute-start.6 = (bf16[2,1024,3,128]{3,1,2,0:T(8,128)(2,1)}, bf16[2,1024,3,128]{3,1,2,0:T(8,128)(2,1)}, u32[]{:S(2)}, u32[]{:S(2)}) collective-permute-start(bf16[2,1024,3,128]{3,1,2,0:T(8,128)(2,1)} %pad_maximum_fusion), channel_id=1, source_target_pairs={{8,0},{16,8},{24,16},{32,24},{40,32},{48,40},{56,48},{64,56},{72,6... | collective-permute-start | bytes 4718600 | tf_op jit(solution)/shard_map/ppermute | solution.py:14
  233.1 13.9 %all-to-all-start.2 = ((bf16[128,24,128]{0,2,1:T(8,128)(2,1)}), bf16[128,24,128]{0,2,1:T(8,128)(2,1)S(1)}, u32[]{:S(2)}, u32[]{:S(2)}) async-start(bf16[128,24,128]{0,2,1:T(8,128)(2,1)} %bitcast.26), calls=%async_computation.2 | async-start | bytes 1572864 | tf_op jit(solution)/shard_map/all_to_all | solution.py:50
  314.2 95.4 %collective-permute-start.7 = (bf16[2,1024,3,128]{3,1,2,0:T(8,128)(2,1)}, bf16[2,1024,3,128]{3,1,2,0:T(8,128)(2,1)}, u32[]{:S(2)}, u32[]{:S(2)}) collective-permute-start(bf16[2,1024,3,128]{3,1,2,0:T(8,128)(2,1)} %pad_maximum_fusion), channel_id=1, source_target_pairs={{16,0},{24,8},{32,16},{40,24},{48,32},{56,40},{64,48},{72,56},{80,... | collective-permute-start | bytes 4718600 | tf_op jit(solution)/shard_map/ppermute | solution.py:14
  347.9 86.8 %collective-permute-start.8 = (bf16[2,1024,3,128]{3,1,2,0:T(8,128)(2,1)}, bf16[2,1024,3,128]{3,1,2,0:T(8,128)(2,1)S(1)}, u32[]{:S(2)}, u32[]{:S(2)}) collective-permute-start(bf16[2,1024,3,128]{3,1,2,0:T(8,128)(2,1)} %pad_maximum_fusion), channel_id=1, source_target_pairs={{24,0},{32,8},{40,16},{48,24},{56,32},{64,40},{72,48},{80,56},{88,... | collective-permute-start | bytes 4718600 | tf_op jit(solution)/shard_map/ppermute | solution.py:14
  381.6 100.2 %collective-permute-start.9 = (bf16[2,1024,3,128]{3,1,2,0:T(8,128)(2,1)}, bf16[2,1024,3,128]{3,1,2,0:T(8,128)(2,1)S(1)}, u32[]{:S(2)}, u32[]{:S(2)}) collective-permute-start(bf16[2,1024,3,128]{3,1,2,0:T(8,128)(2,1)} %pad_maximum_fusion), channel_id=1, source_target_pairs={{32,0},{40,8},{48,16},{56,24},{64,32},{72,40},{80,48},{88,56},{96,... | collective-permute-start | bytes 4718600 | tf_op jit(solution)/shard_map/ppermute | solution.py:14
  385.4 139.7 %collective-permute-start.10 = (bf16[2,1024,3,128]{3,1,2,0:T(8,128)(2,1)}, bf16[2,1024,3,128]{3,1,2,0:T(8,128)(2,1)S(1)}, u32[]{:S(2)}, u32[]{:S(2)}) collective-permute-start(bf16[2,1024,3,128]{3,1,2,0:T(8,128)(2,1)} %pad_maximum_fusion), channel_id=1, source_target_pairs={{40,0},{48,8},{56,16},{64,24},{72,32},{80,40},{88,48},{96,56},{104... | collective-permute-start | bytes 4718600 | tf_op jit(solution)/shard_map/ppermute | solution.py:14
  389.6 270.7 %collective-permute-start.11 = (bf16[2,1024,3,128]{3,1,2,0:T(8,128)(2,1)}, bf16[2,1024,3,128]{3,1,2,0:T(8,128)(2,1)S(1)}, u32[]{:S(2)}, u32[]{:S(2)}) collective-permute-start(bf16[2,1024,3,128]{3,1,2,0:T(8,128)(2,1)} %pad_maximum_fusion), channel_id=1, source_target_pairs={{48,0},{56,8},{64,16},{72,24},{80,32},{88,40},{96,48},{104,56},{11... | collective-permute-start | bytes 4718600 | tf_op jit(solution)/shard_map/ppermute | solution.py:14
  718.3 4.0 copy-start
  770.3 4.0 copy-start
  822.2 4.0 copy-start
  874.1 4.0 copy-start
where the time goes:
time: 928 us; the launch traced here: 927 us
  waiting for transfers between devices  519 us (56%)
  local copies, waits for them, and re-layouts  233 us (25%)
  starting transfers between devices  94.5 us (10%)
  matrix products  42.3 us (5%)
  blocking collectives  19.6 us (2%)
  other arithmetic  18.4 us (2%)
    ppermute x12, waiting for transfers between devices, from_behind(): lax.ppermute(value, axis, [(source, source + steps) for source in range(i...  490 us
    ppermute x12, starting transfers between devices, from_behind(): lax.ppermute(value, axis, [(source, source + steps) for source in range(i...  81 us
    gather x8, local copies, waits for them, and re-layouts, attend_group(): near_keys = key_tiles[neighbor_rows]  78.5 us
    gather x4, local copies, waits for them, and re-layouts, attend_group(): near_values = value_tiles[neighbor_rows]  60.4 us
    dot_general x4, matrix products, attend_group(): jnp.einsum('bhinj,bnjhe->bihe', shares, near_values, preferred_element_ty...  36.2 us
    unnamed x24, local copies, waits for them, and re-layouts  33.1 us
    while x2, local copies, waits for them, and re-layouts, per_device(): lax.map(one_group, (query_tiles.reshape(shard_tiles // group, group, 64,...  27.6 us
    all_to_all x1, blocking collectives, per_device(): lax.all_to_all(mixed, 'uly', split_axis=0, concat_axis=1, tiled=True)  19.6 us
  transfers between devices with their start and end apart: 15, of which 12 were waited for; matrix products, arithmetic and copies ran while one was open for 4% of the time, Pallas kernels for 0%

commit v1 on v0

v1 whole, which is shorter than its diff:
```python
import functools
import math

import jax
import jax.numpy as jnp
from jax import lax
from jax.experimental import pallas as pl
from jax.experimental.pallas import tpu as pltpu
from jax.sharding import PartitionSpec as P

MESH = pl.DeviceIdType.MESH
TILE = 64
WIDE = 20
FRAME = 60
REACH = 6
GROUP = 2
SPAN = (GROUP + 2) * TILE
CENTRES = tuple(FRAME * t + WIDE * h for t in (-1, 0, 1) for h in (-1, 0, 1))
NEAR = (3, 4, 5)
MIDDLE = (1, 2, 6, 7)
FAR = (0, 8)


def kernel(
    blocks, peers, heads,
    neighbors, counts, queries, keys, values, query_gain, key_gain,
    out,
    kv, queries_in, keys_out, queries_out, total, acc, mask, mixed,
    uly_send, uly_recv, ring_send, ring_recv, pair_send, pair_recv, back_send, back_recv,
):
    tokens = queries.shape[0]
    hd = query_gain.shape[1]
    block = tokens * peers
    tiles = block // TILE
    cfg, me, mine = lax.axis_index("cfg"), lax.axis_index("blk"), lax.axis_index("uly")
    core = lax.rem(me, 2)
    above, below = lax.rem(me + 2, blocks), lax.rem(me + blocks - 2, blocks)
    pair = me + 1 - 2 * core
    scale = hd ** -0.5 * math.log2(math.e)

    def at_blk(b):
        return (cfg, b, mine)

    def at_uly(u):
        return (cfg, me, u)

    def partner(d):
        return lax.rem(mine + d, peers)

    barrier = pltpu.get_barrier_semaphore()
    for b in (above, below, pair):
        pl.semaphore_signal(barrier, inc=1, device_id=at_blk(b), device_id_type=MESH)
    for d in range(1, peers):
        pl.semaphore_signal(barrier, inc=1, device_id=at_uly(partner(d)), device_id_type=MESH)
    pl.semaphore_wait(barrier, 3 + peers - 1)

    own = REACH * block

    def columns(u, h):
        return pl.ds(pl.multiple_of((u * heads + h) * hd, hd), hd)

    def my_rows(start):
        return pl.ds(pl.multiple_of(start + mine * tokens, tokens), tokens)

    def normed(states, gain, u, h):
        wide = states[:, columns(u, h)].astype(jnp.float32)
        factor = lax.rsqrt(jnp.mean(wide * wide, axis=-1, keepdims=True) + 1e-06)
        return (wide * factor * gain[...]).astype(jnp.bfloat16)

    def spread(kind, h):
        if kind == 2:
            landing = queries_in.at[h, my_rows(0), :]
            queries_in[h, my_rows(0), :] = normed(queries, query_gain, mine, h)
        elif kind == 1:
            landing = kv.at[h, 1, my_rows(own), :]
            kv[h, 1, my_rows(own), :] = values[:, columns(mine, h)]
        else:
            landing = kv.at[h, 0, my_rows(own), :]
            kv[h, 0, my_rows(own), :] = normed(keys, key_gain, mine, h)

        def send(d, carry):
            u = partner(d)
            if kind == 2:
                queries_out[h, u] = normed(queries, query_gain, u, h)
                source = queries_out.at[h, u]
            elif kind == 1:
                source = values.at[:, columns(u, h)]
            else:
                keys_out[h, u] = normed(keys, key_gain, u, h)
                source = keys_out.at[h, u]
            pltpu.make_async_remote_copy(
                source, landing, uly_send.at[kind, h], uly_recv.at[kind, h],
                device_id=at_uly(u), device_id_type=MESH,
            ).start()
            return carry

        lax.fori_loop(1, peers, send, 0)

    rest = (peers - 1) * tokens

    def wait_bytes(ref, sem):
        pltpu.make_async_copy(ref, ref, sem).wait()

    def wait_spread(kind, h):
        ref = queries_in.at[h, pl.ds(0, rest), :] if kind == 2 else kv.at[h, kind, pl.ds(own, rest), :]
        wait_bytes(ref, uly_recv.at[kind, h])

    sent = []

    def ring(unit, slot, source, target, rows, to):
        h, which = unit
        copy = pltpu.make_async_remote_copy(
            kv.at[h, which, pl.ds(source, rows), :], kv.at[h, which, pl.ds(target, rows), :],
            ring_send.at[h, which, slot], ring_recv.at[h, which, slot],
            device_id=at_blk(to), device_id_type=MESH,
        )
        copy.start()
        sent.append(copy)
        return copy

    def share(unit, slot, source):
        h, which = unit
        target = pl.multiple_of(source + (2 * core - 1) * block, block)
        copy = pltpu.make_async_remote_copy(
            kv.at[h, which, pl.ds(source, block), :], kv.at[h, which, pl.ds(target, block), :],
            pair_send.at[h, which, slot], pair_recv.at[h, which, slot],
            device_id=at_blk(pair), device_id_type=MESH,
        )
        copy.start()
        sent.append(copy)
        return copy

    units = [(h, which) for h in range(heads) for which in (1, 0)]
    n_units = len(units)
    ringed, shared = {}, {}

    def step(k):
        if k < n_units:
            unit = units[k]
            wait_spread(unit[1], unit[0])
            ringed[k, 0] = ring(unit, 0, own, own - 2 * block, block, above)
            ringed[k, 1] = ring(unit, 1, own, own + 2 * block, block, below)
            shared[k, 0] = share(unit, 0, own)
        n = k - 1
        if 0 <= n < n_units:
            unit = units[n]
            ringed[n, 0].wait_recv()
            ringed[n, 2] = ring(unit, 2, own - 2 * block, own - 4 * block, block, above)
            ringed[n, 1].wait_recv()
            ringed[n, 3] = ring(unit, 3, own + 2 * block, own + 4 * block, block, below)
            shared[n, 1] = share(unit, 1, own - 2 * block)
            shared[n, 2] = share(unit, 2, own + 2 * block)
        n = k - 2
        if 0 <= n < n_units:
            unit = units[n]
            ringed[n, 2].wait_recv()
            ringed[n, 3].wait_recv()
            ringed[n, 4] = ring(
                unit, 4,
                pl.multiple_of(own + (4 - 8 * core) * block, block),
                pl.multiple_of(own + (6 - 12 * core) * block, block),
                block, lax.rem(me + blocks + 4 * core - 2, blocks),
            )
            ringed[n, 5] = ring(
                unit, 5,
                pl.multiple_of(own - 3 * block - TILE + core * (7 * block + TILE), TILE),
                pl.multiple_of(own - 5 * block - TILE + core * (11 * block + TILE), TILE),
                TILE, lax.rem(me + blocks + 2 - 4 * core, blocks),
            )
            shared[n, 3] = share(unit, 3, own - 4 * block)
            shared[n, 4] = share(unit, 4, own + 4 * block)
        n = k - 3
        if 0 <= n < n_units:
            unit = units[n]
            ringed[n, 4].wait_recv()
            ringed[n, 5].wait_recv()
            shared[n, 5] = share(unit, 5, pl.multiple_of(own + (6 - 12 * core) * block, block))

    def build_mask():
        shape = (16, SPAN)
        row = lax.broadcasted_iota(jnp.int32, shape, 0)
        place = lax.broadcasted_iota(jnp.int32, shape, 1) // TILE
        centre = (row // 3 - 1) * FRAME + (row % 3 - 1) * WIDE

        def one(t, carry):
            tile = centre + place + (me * tiles + t - 1 - lax.rem(t, GROUP))
            live = jnp.zeros(shape, jnp.float32)
            count = counts[0, t]
            for n in range(neighbors.shape[1]):
                entry = jnp.where(n < count, neighbors[t, n], -(2 ** 20))
                live = jnp.where(tile == entry, 1.0, live)
            mask[t] = live
            return carry

        lax.fori_loop(0, tiles, one, 0)

    def attend(h, windows, first=False, last=False):
        rows = GROUP * TILE

        def group(g, carry):
            t = g * GROUP
            mine_rows = pl.ds(pl.multiple_of(t * TILE, rows), rows)
            q = queries_in[h, mine_rows, :]
            if first:
                sums = jnp.zeros((rows, 128), jnp.float32)
                result = jnp.zeros((rows, hd), jnp.float32)
            else:
                sums = total[h, mine_rows, :]
                result = acc[h, mine_rows, :]
            for w in windows:
                near = pl.ds(pl.multiple_of(own + (t + CENTRES[w] - 1) * TILE, TILE), SPAN)
                scores = lax.dot_general(
                    q, kv[h, 0, near, :], (((1,), (1,)), ((), ())), preferred_element_type=jnp.float32
                )
                weights = jnp.exp2(scores * scale)
                live = jnp.concatenate(
                    [jnp.broadcast_to(mask[t + a, pl.ds(w, 1), :], (TILE, SPAN)) for a in range(GROUP)], axis=0
                )
                weights = weights * live
                for part in range(0, SPAN, 128):
                    sums = sums + weights[:, part : part + 128]
                result = result + jnp.dot(
                    weights.astype(jnp.bfloat16), kv[h, 1, near, :], preferred_element_type=jnp.float32
                )
            if last:
                mixed[h, mine_rows, :] = (result / jnp.sum(sums, axis=-1, keepdims=True)).astype(jnp.bfloat16)
            else:
                total[h, mine_rows, :] = sums
                acc[h, mine_rows, :] = result
            return carry

        lax.fori_loop(0, tiles // GROUP, group, 0)

    def near_part(h):
        wait_spread(2, h)
        for which in (1, 0):
            n = units.index((h, which))
            for slot in (0, 1, 2):
                shared[n, slot].wait_recv()
        attend(h, NEAR, first=True)

    def middle_part(h):
        for which in (1, 0):
            n = units.index((h, which))
            for slot in (3, 4):
                shared[n, slot].wait_recv()
        attend(h, MIDDLE)

    def far_part(h):
        for which in (1, 0):
            shared[units.index((h, which)), 5].wait_recv()
        attend(h, FAR, last=True)
        landing = out.at[:, columns(mine, h)]

        def send(d, carry):
            u = partner(d)
            pltpu.make_async_remote_copy(
                mixed.at[h, pl.ds(pl.multiple_of(u * tokens, tokens), tokens), :], landing,
                back_send.at[h], back_recv.at[h], device_id=at_uly(u), device_id_type=MESH,
            ).start()
            return carry

        lax.fori_loop(1, peers, send, 0)
        out[:, columns(mine, h)] = mixed[h, my_rows(0), :]

    for h in range(heads):
        spread(1, h)
        spread(0, h)
    for h in range(heads):
        spread(2, h)
    step(0)
    step(1)
    build_mask()
    step(2)
    for k in range(3, n_units + 3):
        step(k)
        if k % 2 == 1:
            h = (k - 3) // 2
            if h >= 1:
                far_part(h - 1)
            near_part(h)
        else:
            middle_part((k - 4) // 2)
    far_part(heads - 1)

    for copy in sent:
        copy.wait_send()
    for h in range(heads):
        for kind in range(3):
            wait_bytes(queries_in.at[h, pl.ds(0, rest), :], uly_send.at[kind, h])
        wait_bytes(queries_in.at[h, pl.ds(0, rest), :], back_send.at[h])
        wait_bytes(queries_in.at[h, pl.ds(0, rest), :], back_recv.at[h])


def solution(mesh):
    blocks, peers = mesh.shape["blk"], mesh.shape["uly"]

    def per_device(queries, keys, values, query_gain, key_gain, neighbors, counts):
        tokens, width = queries.shape
        hd = query_gain.shape[0]
        heads = width // hd // peers
        block = tokens * peers
        tiles = block // TILE
        vmem = pl.BlockSpec(memory_space=pltpu.VMEM)
        smem = pl.BlockSpec(memory_space=pltpu.SMEM)
        dma = pltpu.SemaphoreType.DMA
        return pl.pallas_call(
            functools.partial(kernel, blocks, peers, heads),
            out_shape=jax.ShapeDtypeStruct((tokens, width), jnp.bfloat16),
            in_specs=[smem, smem] + [vmem] * 5,
            out_specs=vmem,
            scratch_shapes=[
                pltpu.VMEM((heads, 2, (2 * REACH + 1) * block, hd), jnp.bfloat16),
                pltpu.VMEM((heads, block, hd), jnp.bfloat16),
                pltpu.VMEM((heads, peers, tokens, hd), jnp.bfloat16),
                pltpu.VMEM((heads, peers, tokens, hd), jnp.bfloat16),
                pltpu.VMEM((heads, block, 128), jnp.float32),
                pltpu.VMEM((heads, block, hd), jnp.float32),
                pltpu.VMEM((tiles, 16, SPAN), jnp.float32),
                pltpu.VMEM((heads, block, hd), jnp.bfloat16),
                dma((3, heads)), dma((3, heads)),
                dma((heads, 2, 6)), dma((heads, 2, 6)),
                dma((heads, 2, 6)), dma((heads, 2, 6)),
                dma((heads,)), dma((heads,)),
            ],
            compiler_params=pltpu.CompilerParams(
                collective_id=0, has_side_effects=True, vmem_limit_bytes=56 * 2 ** 20
            ),
        )(neighbors, counts.reshape(1, -1), queries, keys, values, query_gain.reshape(1, -1), key_gain.reshape(1, -1))

    tokens = P(("cfg", "blk", "uly"), None)
    return jax.shard_map(
        per_device,
        mesh=mesh,
        in_specs=(tokens, tokens, tokens, P(), P(), P("blk", None), P("blk")),
        out_specs=tokens,
        check_vma=False,
    )
```

time: 928 us -> 126 us (0.14)
  the two profiles are of different devices: /device:TPU:64 before, /device:TPU:1 now
where the time goes in v1:
time: 126 us
  Pallas kernels  124 us (98%)
  local copies, waits for them, and re-layouts  2.06 us (2%)
    pallas_call x1, Pallas kernels, per_device(): pl.pallas_call(functools.partial(kernel, blocks, peers, heads), out_shape...  124 us

profile of v1, /device:TPU:1, one launch (start us, length us, event | category | flops | bytes accessed | tf_op | source)
XLA Modules:
  0.0 125.6 jit_solution(15354271158515629892)
XLA Ops:
  0.0 123.6 %shard_map.73 = bf16[128,3072]{1,0:T(8,128)(2,1)} custom-call(s32[16,27]{1,0:T(8,128)} %neighbors.1, s32[1,16]{1,0:T(1,128)} %bitcast.3, bf16[128,3072]{1,0:T(8,128)(2,1)} %queries.1, bf16[128,3072]{1,0:T(8,128)(2,1)} %keys.1, bf16[128,3072]{1,0:T(8,128)(2,1)} %values.1, f32[1,128]{1,0:T(1,128)} %bitcast.4, f32[1,128]{1,0:T(1,128)} %bitcast.5), custom_call_target="tpu_custom_call" | custom-call | tf_op jit(solution)/shard_map/pallas_call | solution.py:307
  123.6 2.1 %copy.9 = bf16[128,3072]{1,0:T(8,128)(2,1)} copy(bf16[128,3072]{1,0:T(8,128)(2,1)} %shard_map.73) | data formatting | bytes 1572864

commit v2 on v1

v2 whole, which is shorter than its diff:
```python
import functools
import math

import jax
import jax.numpy as jnp
from jax import lax
from jax.experimental import pallas as pl
from jax.experimental.pallas import tpu as pltpu
from jax.sharding import PartitionSpec as P

MESH = pl.DeviceIdType.MESH
TILE = 64
WIDE = 20
FRAME = 60
REACH = 6
GROUP = 2
SPAN = (GROUP + 2) * TILE
CENTRES = tuple(FRAME * t + WIDE * h for t in (-1, 0, 1) for h in (-1, 0, 1))
NEAR = (3, 4, 5)
MIDDLE = (1, 2, 6, 7)
FAR = (0, 8)


PIECES = (1, 5, 4, 4, 2)
LOWER_FIRST = (0, 1, 6, 10, 14)
UPPER_FIRST = (15, 0, 5, 9, 13)
EARLY = 2


def kernel(
    blocks, peers, heads,
    neighbors, counts, queries_hbm, keys_hbm, values_hbm, query_gain, key_gain,
    out,
    queries, keys, values, kv, queries_in, keys_out, queries_out, total, acc, mask, mixed,
    load_sem, uly_send, uly_recv, early_recv, ring_send, ring_recv, pair_send, pair_recv,
    tail_send, tail_recv, tail_pair_send, tail_pair_recv, back_send, back_recv, own_sem,
):
    tokens = queries.shape[0]
    hd = query_gain.shape[1]
    block = tokens * peers
    tiles = block // TILE
    cfg, me, mine = lax.axis_index("cfg"), lax.axis_index("blk"), lax.axis_index("uly")
    core = lax.rem(me, 2)
    above, below = lax.rem(me + 2, blocks), lax.rem(me + blocks - 2, blocks)
    pair = me + 1 - 2 * core
    scale = hd ** -0.5 * math.log2(math.e)

    def at_blk(b):
        return (cfg, b, mine)

    def at_uly(u):
        return (cfg, me, u)

    def partner(d):
        return lax.rem(mine + d, peers)

    barrier = pltpu.get_barrier_semaphore()
    for d in range(1, peers):
        pl.semaphore_signal(barrier, inc=1, device_id=at_uly(partner(d)), device_id_type=MESH)
    for b in (above, below, pair):
        pl.semaphore_signal(barrier, inc=1, device_id=at_blk(b), device_id_type=MESH)

    loads = [
        pltpu.make_async_copy(source, target, load_sem.at[i])
        for i, (source, target) in enumerate(((keys_hbm, keys), (values_hbm, values), (queries_hbm, queries)))
    ]
    for load in loads:
        load.start()

    own = REACH * block

    def columns(u, h):
        return pl.ds(pl.multiple_of((u * heads + h) * hd, hd), hd)

    def rows_of(start, u):
        return pl.ds(pl.multiple_of(start + u * tokens, tokens), tokens)

    def normed(states, gain, u, h):
        wide = states[:, columns(u, h)].astype(jnp.float32)
        factor = lax.rsqrt(jnp.mean(wide * wide, axis=-1, keepdims=True) + 1e-06)
        return (wide * factor * gain[...]).astype(jnp.bfloat16)

    def norm(kind, h):
        states, gain, target = (queries, query_gain, queries_out) if kind == 2 else (keys, key_gain, keys_out)

        def one(u, carry):
            target[h, u] = normed(states, gain, u, h)
            return carry

        lax.fori_loop(0, peers, one, 0)

    def spread(kind, h):
        n = units.index((h, kind)) if kind < 2 else None
        if kind == 2:
            landing = queries_in.at[h, rows_of(0, mine), :]
            queries_in[h, rows_of(0, mine), :] = queries_out[h, mine]
        elif kind == 1:
            landing = kv.at[h, 1, rows_of(own, mine), :]
            kv[h, 1, rows_of(own, mine), :] = values[:, columns(mine, h)]
        else:
            landing = kv.at[h, 0, rows_of(own, mine), :]
            kv[h, 0, rows_of(own, mine), :] = keys_out[h, mine]

        def send(d, carry):
            u = partner(d)
            if kind == 2:
                source = queries_out.at[h, u]
            elif kind == 1:
                source = values.at[:, columns(u, h)]
            else:
                source = keys_out.at[h, u]
            arrival = early_recv.at[n, d] if n is not None and n < EARLY else uly_recv.at[kind, h]
            pltpu.make_async_remote_copy(
                source, landing, uly_send.at[kind, h], arrival, device_id=at_uly(u), device_id_type=MESH,
            ).start()
            return carry

        lax.fori_loop(1, peers, send, 0)

    rest = (peers - 1) * tokens

    def wait_bytes(ref, sem):
        pltpu.make_async_copy(ref, ref, sem).wait()

    def wait_spread(kind, h):
        ref = queries_in.at[h, pl.ds(0, rest), :] if kind == 2 else kv.at[h, kind, pl.ds(own, rest), :]
        wait_bytes(ref, uly_recv.at[kind, h])

    sent = []

    def remote(unit, source, target, rows, send, recv, to):
        h, which = unit
        copy = pltpu.make_async_remote_copy(
            kv.at[h, which, pl.ds(source, rows), :], kv.at[h, which, pl.ds(target, rows), :],
            send, recv, device_id=at_blk(to), device_id_type=MESH,
        )
        copy.start()
        sent.append(copy)
        return copy

    def ring(unit, slot, source, target, rows, to):
        return remote(unit, source, target, rows, ring_send.at[(*unit, slot)], ring_recv.at[(*unit, slot)], to)

    def share(unit, slot, source):
        target = pl.multiple_of(source + (2 * core - 1) * block, block)
        return remote(unit, source, target, block, pair_send.at[(*unit, slot)], pair_recv.at[(*unit, slot)], pair)

    units = [(h, which) for h in range(heads) for which in (1, 0)]
    n_units = len(units)
    ringed, shared = {}, {}

    def own_in_pieces(k):
        h, which = unit = units[k]

        def forward(u):
            for slot, target, to in ((0, own - 2 * block, above), (1, own + 2 * block, below)):
                pltpu.make_async_remote_copy(
                    kv.at[h, which, rows_of(own, u), :], kv.at[h, which, rows_of(target, u), :],
                    ring_send.at[h, which, slot], ring_recv.at[h, which, slot],
                    device_id=at_blk(to), device_id_type=MESH,
                ).start()

        def one(d, carry):
            u = lax.rem(mine + peers - d, peers)
            wait_bytes(kv.at[h, which, rows_of(own, u), :], early_recv.at[k, d])
            forward(u)
            return carry

        forward(mine)
        lax.fori_loop(1, peers, one, 0)
        for slot, target, to in ((0, own - 2 * block, above), (1, own + 2 * block, below)):
            ringed[k, slot] = pltpu.make_async_remote_copy(
                kv.at[h, which, pl.ds(own, block), :], kv.at[h, which, pl.ds(target, block), :],
                ring_send.at[h, which, slot], ring_recv.at[h, which, slot],
                device_id=at_blk(to), device_id_type=MESH,
            )
            sent.append(ringed[k, slot])
        shared[k, 0] = share(unit, 0, own)

    far_source = own + (4 - 8 * core) * block
    far_target = own + (6 - 12 * core) * block
    far_to = lax.rem(me + blocks + 4 * core - 2, blocks)

    def piece_start(i):
        return (LOWER_FIRST[i] + core * (UPPER_FIRST[i] - LOWER_FIRST[i])) * TILE

    def step_own(k):
        if k < EARLY:
            own_in_pieces(k)
        elif k < n_units:
            unit = units[k]
            wait_spread(unit[1], unit[0])
            ringed[k, 0] = ring(unit, 0, own, own - 2 * block, block, above)
            ringed[k, 1] = ring(unit, 1, own, own + 2 * block, block, below)
            shared[k, 0] = share(unit, 0, own)

    def step_next(n):
        if not 0 <= n < n_units:
            return
        unit = units[n]
        ringed[n, 0].wait_recv()
        ringed[n, 2] = ring(unit, 2, own - 2 * block, own - 4 * block, block, above)
        ringed[n, 1].wait_recv()
        ringed[n, 3] = ring(unit, 3, own + 2 * block, own + 4 * block, block, below)
        shared[n, 1] = share(unit, 1, own - 2 * block)
        shared[n, 2] = share(unit, 2, own + 2 * block)

    def step_far(n):
        if not 0 <= n < n_units:
            return
        unit = units[n]
        ringed[n, 2].wait_recv()
        ringed[n, 3].wait_recv()
        ringed[n, 5] = ring(
            unit, 5,
            pl.multiple_of(own - 3 * block - TILE + core * (7 * block + TILE), TILE),
            pl.multiple_of(own - 5 * block - TILE + core * (11 * block + TILE), TILE),
            TILE, lax.rem(me + blocks + 2 - 4 * core, blocks),
        )
        if n == n_units - 1:
            for i, size in enumerate(PIECES):
                start = piece_start(i)
                ringed[n, 6 + i] = remote(
                    unit, pl.multiple_of(far_source + start, TILE), pl.multiple_of(far_target + start, TILE),
                    size * TILE, tail_send.at[i], tail_recv.at[i], far_to,
                )
        else:
            ringed[n, 4] = ring(
                unit, 4, pl.multiple_of(far_source, block), pl.multiple_of(far_target, block), block, far_to
            )
        shared[n, 3] = share(unit, 3, own - 4 * block)
        shared[n, 4] = share(unit, 4, own + 4 * block)

    def step_last(n):
        if not 0 <= n < n_units - 1:
            return
        ringed[n, 5].wait_recv()
        ringed[n, 4].wait_recv()
        shared[n, 5] = share(units[n], 5, pl.multiple_of(far_target, block))

    def share_piece(i):
        n = n_units - 1
        ringed[n, 6 + i].wait_recv()
        source = pl.multiple_of(far_target + piece_start(i), TILE)
        target = pl.multiple_of(far_target + piece_start(i) + (2 * core - 1) * block, TILE)
        shared[n, 6 + i] = remote(
            units[n], source, target, PIECES[i] * TILE, tail_pair_send.at[i], tail_pair_recv.at[i], pair
        )

    def build_mask():
        shape = (16, SPAN)
        row = lax.broadcasted_iota(jnp.int32, shape, 0)
        place = lax.broadcasted_iota(jnp.int32, shape, 1) // TILE
        centre = (row // 3 - 1) * FRAME + (row % 3 - 1) * WIDE

        def one(t, carry):
            tile = centre + place + (me * tiles + t - 1 - lax.rem(t, GROUP))
            live = jnp.zeros(shape, jnp.float32)
            count = counts[0, t]
            for n in range(neighbors.shape[1]):
                entry = jnp.where(n < count, neighbors[t, n], -(2 ** 20))
                live = jnp.where(tile == entry, 1.0, live)
            mask[t] = live
            return carry

        lax.fori_loop(0, tiles, one, 0)

    def attend(h, windows, first=False, last=False, begin=0, end=None):
        rows = GROUP * TILE

        def group(g, carry):
            t = g * GROUP
            mine_rows = pl.ds(pl.multiple_of(t * TILE, rows), rows)
            q = queries_in[h, mine_rows, :]
            if first:
                sums = jnp.zeros((rows, 128), jnp.float32)
                result = jnp.zeros((rows, hd), jnp.float32)
            else:
                sums = total[h, mine_rows, :]
                result = acc[h, mine_rows, :]

            def near(w):
                return pl.ds(pl.multiple_of(own + (t + CENTRES[w] - 1) * TILE, TILE), SPAN)

            def score(w):
                return lax.dot_general(
                    q, kv[h, 0, near(w), :], (((1,), (1,)), ((), ())), preferred_element_type=jnp.float32
                )

            scores = score(windows[0])
            for i, w in enumerate(windows):
                coming = score(windows[i + 1]) if i + 1 < len(windows) else None
                live = jnp.concatenate(
                    [jnp.broadcast_to(mask[t + a, pl.ds(w, 1), :], (TILE, SPAN)) for a in range(GROUP)], axis=0
                )
                weights = jnp.exp2(scores * scale) * live
                for part in range(0, SPAN, 128):
                    sums = sums + weights[:, part : part + 128]
                result = result + jnp.dot(
                    weights.astype(jnp.bfloat16), kv[h, 1, near(w), :], preferred_element_type=jnp.float32
                )
                scores = coming
            if last:
                mixed[h, mine_rows, :] = (result / jnp.sum(sums, axis=-1, keepdims=True)).astype(jnp.bfloat16)
            else:
                total[h, mine_rows, :] = sums
                acc[h, mine_rows, :] = result
            return carry

        lax.fori_loop(begin, tiles // GROUP if end is None else end, group, 0, unroll=2)

    def near_part(h):
        wait_spread(2, h)
        for which in (1, 0):
            n = units.index((h, which))
            for slot in (0, 1, 2):
                shared[n, slot].wait_recv()
        attend(h, NEAR, first=True)

    def middle_waits(h):
        for which in (1, 0):
            n = units.index((h, which))
            for slot in (3, 4):
                shared[n, slot].wait_recv()

    def middle_part(h):
        middle_waits(h)
        attend(h, MIDDLE)

    def send_back(h, u):
        source = mixed.at[h, rows_of(0, u), :]
        landing = out.at[:, columns(mine, h)]

        @pl.when(u != mine)
        def _():
            pltpu.make_async_remote_copy(
                source, landing, back_send.at[h], back_recv.at[h], device_id=at_uly(u), device_id_type=MESH,
            ).start()

        @pl.when(u == mine)
        def _():
            pltpu.make_async_copy(source, landing, own_sem.at[h]).start()

    def far_part(h):
        for which in (1, 0):
            shared[units.index((h, which)), 5].wait_recv()
        attend(h, FAR, last=True)

        def send(u, carry):
            send_back(h, u)
            return carry

        lax.fori_loop(0, peers, send, 0)

    loads[0].wait()
    norm(0, 0)
    loads[1].wait()
    pl.semaphore_wait(barrier, 3 + peers - 1)
    spread(1, 0)
    spread(0, 0)
    step_own(0)
    norm(0, 1)
    spread(1, 1)
    spread(0, 1)
    step_own(1)
    norm(0, 2)
    spread(1, 2)
    spread(0, 2)
    step_next(0)
    loads[2].wait()
    for h in range(heads):
        norm(2, h)
        spread(2, h)
    build_mask()
    last_head = heads - 1
    for k in range(2, n_units + 2):
        step_own(k)
        step_next(k - 1)
        step_far(k - 2)
        if k == n_units + 1:
            break
        step_last(k - 3)
        if k == 3:
            near_part(0)
        elif k == 4:
            middle_part(0)
        elif k == 5:
            far_part(0)
            near_part(1)
        elif k == 6:
            middle_part(1)
            near_part(2)
    n = n_units - 1
    far_part(last_head - 1)
    step_last(n_units - 2)
    middle_waits(last_head)
    half = tiles // GROUP // 2
    attend(last_head, MIDDLE, begin=0, end=half)
    ringed[n, 5].wait_recv()
    for i in (0, 1):
        share_piece(i)
    attend(last_head, MIDDLE, begin=half)
    for i in (2, 3, 4):
        share_piece(i)
    shared[units.index((last_head, 1)), 5].wait_recv()
    shared[n, 6].wait_recv()
    for i in range(1, len(PIECES)):
        shared[n, 6 + i].wait_recv()
        attend(last_head, FAR, last=True, begin=2 * i - 2, end=2 * i)
        for u in (2 * i - 2, 2 * i - 1):
            send_back(last_head, u)

    for copy in sent:
        copy.wait_send()
    for h in range(heads):
        for kind in range(3):
            wait_bytes(queries_in.at[h, pl.ds(0, rest), :], uly_send.at[kind, h])
        wait_bytes(queries_in.at[h, pl.ds(0, rest), :], back_send.at[h])
        wait_bytes(queries_in.at[h, pl.ds(0, tokens), :], own_sem.at[h])
    for h in range(heads):
        wait_bytes(queries_in.at[h, pl.ds(0, rest), :], back_recv.at[h])


def solution(mesh):
    blocks, peers = mesh.shape["blk"], mesh.shape["uly"]

    def per_device(queries, keys, values, query_gain, key_gain, neighbors, counts):
        tokens, width = queries.shape
        hd = query_gain.shape[0]
        heads = width // hd // peers
        block = tokens * peers
        tiles = block // TILE
        vmem = pl.BlockSpec(memory_space=pltpu.VMEM)
        smem = pl.BlockSpec(memory_space=pltpu.SMEM)
        dma = pltpu.SemaphoreType.DMA
        return pl.pallas_call(
            functools.partial(kernel, blocks, peers, heads),
            out_shape=jax.ShapeDtypeStruct((tokens, width), jnp.bfloat16),
            in_specs=[smem, smem] + [pl.BlockSpec(memory_space=pl.ANY)] * 3 + [vmem] * 2,
            out_specs=pl.BlockSpec(memory_space=pl.ANY),
            scratch_shapes=[
                pltpu.VMEM((tokens, width), jnp.bfloat16),
                pltpu.VMEM((tokens, width), jnp.bfloat16),
                pltpu.VMEM((tokens, width), jnp.bfloat16),
                pltpu.VMEM((heads, 2, (2 * REACH + 1) * block, hd), jnp.bfloat16),
                pltpu.VMEM((heads, block, hd), jnp.bfloat16),
                pltpu.VMEM((heads, peers, tokens, hd), jnp.bfloat16),
                pltpu.VMEM((heads, peers, tokens, hd), jnp.bfloat16),
                pltpu.VMEM((heads, block, 128), jnp.float32),
                pltpu.VMEM((heads, block, hd), jnp.float32),
                pltpu.VMEM((tiles, 16, SPAN), jnp.float32),
                pltpu.VMEM((heads, block, hd), jnp.bfloat16),
                dma((3,)), dma((3, heads)), dma((3, heads)), dma((EARLY, peers)),
                dma((heads, 2, 6)), dma((heads, 2, 6)),
                dma((heads, 2, 6)), dma((heads, 2, 6)),
                dma((len(PIECES),)), dma((len(PIECES),)), dma((len(PIECES),)), dma((len(PIECES),)),
                dma((heads,)), dma((heads,)), dma((heads,)),
            ],
            compiler_params=pltpu.CompilerParams(
                collective_id=0, has_side_effects=True, vmem_limit_bytes=56 * 2 ** 20
            ),
        )(neighbors, counts.reshape(1, -1), queries, keys, values, query_gain.reshape(1, -1), key_gain.reshape(1, -1))

    tokens = P(("cfg", "blk", "uly"), None)
    return jax.shard_map(
        per_device,
        mesh=mesh,
        in_specs=(tokens, tokens, tokens, P(), P(), P("blk", None), P("blk")),
        out_specs=tokens,
        check_vma=False,
    )
```

time: 126 us -> 111 us (0.88)
  Pallas kernels: 124 us -> 108 us
    pallas_call x1, Pallas kernels: 124 us -> 108 us  [per_device(): pl.pallas_call(functools.partial(kernel, blocks, peers, heads), out_shape...]
where the time goes in v2:
time: 111 us; the launch traced here: 110 us
  Pallas kernels  108 us (97%)
  local copies, waits for them, and re-layouts  2.06 us (2%)
    pallas_call x1, Pallas kernels, per_device(): pl.pallas_call(functools.partial(kernel, blocks, peers, heads), out_shape...  108 us

profile of v2, /device:TPU:1, one launch (start us, length us, event | category | flops | bytes accessed | tf_op | source)
XLA Modules:
  0.0 109.9 jit_solution(17435403844845844747)
XLA Ops:
  0.0 107.8 %shard_map.73 = bf16[128,3072]{1,0:T(8,128)(2,1)} custom-call(s32[16,27]{1,0:T(8,128)} %neighbors.1, s32[1,16]{1,0:T(1,128)} %bitcast.3, bf16[128,3072]{1,0:T(8,128)(2,1)} %queries_hbm.1, bf16[128,3072]{1,0:T(8,128)(2,1)} %keys_hbm.1, bf16[128,3072]{1,0:T(8,128)(2,1)} %values_hbm.1, f32[1,128]{1,0:T(1,128)} %bitcast.4, f32[1,128]{1,0:T(1,128)} %bitcast.5), custom_call_target="tpu_custom_call" | custom-call | tf_op jit(solution)/shard_map/pallas_call | solution.py:436
  107.8 2.1 %copy.9 = bf16[128,3072]{1,0:T(8,128)(2,1)} copy(bf16[128,3072]{1,0:T(8,128)(2,1)} %shard_map.73) | data formatting | bytes 1572864

commit v3 on v2

--- a/solution.py
+++ b/solution.py
@@ -24,7 +24,6 @@
 PIECES = (1, 5, 4, 4, 2)
 LOWER_FIRST = (0, 1, 6, 10, 14)
 UPPER_FIRST = (15, 0, 5, 9, 13)
-EARLY = 2
 
 
 def kernel(
@@ -32,7 +31,7 @@
     neighbors, counts, queries_hbm, keys_hbm, values_hbm, query_gain, key_gain,
     out,
     queries, keys, values, kv, queries_in, keys_out, queries_out, total, acc, mask, mixed,
-    load_sem, uly_send, uly_recv, early_recv, ring_send, ring_recv, pair_send, pair_recv,
+    load_sem, uly_send, uly_recv, piece_recv, ring_send, ring_recv, pair_send, pair_recv,
     tail_send, tail_recv, tail_pair_send, tail_pair_recv, back_send, back_recv, own_sem,
 ):
     tokens = queries.shape[0]
@@ -90,16 +89,11 @@
         lax.fori_loop(0, peers, one, 0)
 
     def spread(kind, h):
-        n = units.index((h, kind)) if kind < 2 else None
         if kind == 2:
             landing = queries_in.at[h, rows_of(0, mine), :]
             queries_in[h, rows_of(0, mine), :] = queries_out[h, mine]
-        elif kind == 1:
-            landing = kv.at[h, 1, rows_of(own, mine), :]
-            kv[h, 1, rows_of(own, mine), :] = values[:, columns(mine, h)]
         else:
-            landing = kv.at[h, 0, rows_of(own, mine), :]
-            kv[h, 0, rows_of(own, mine), :] = keys_out[h, mine]
+            landing = kv.at[h, kind, rows_of(own, mine), :]
 
         def send(d, carry):
             u = partner(d)
@@ -109,7 +103,7 @@
                 source = values.at[:, columns(u, h)]
             else:
                 source = keys_out.at[h, u]
-            arrival = early_recv.at[n, d] if n is not None and n < EARLY else uly_recv.at[kind, h]
+            arrival = uly_recv.at[h] if kind == 2 else piece_recv.at[h, kind, d]
             pltpu.make_async_remote_copy(
                 source, landing, uly_send.at[kind, h], arrival, device_id=at_uly(u), device_id_type=MESH,
             ).start()
@@ -121,10 +115,6 @@
 
     def wait_bytes(ref, sem):
         pltpu.make_async_copy(ref, ref, sem).wait()
-
-    def wait_spread(kind, h):
-        ref = queries_in.at[h, pl.ds(0, rest), :] if kind == 2 else kv.at[h, kind, pl.ds(own, rest), :]
-        wait_bytes(ref, uly_recv.at[kind, h])
 
     sent = []
 
@@ -149,24 +139,37 @@
     n_units = len(units)
     ringed, shared = {}, {}
 
-    def own_in_pieces(k):
+    def forward(unit, u):
+        h, which = unit
+        for slot, target, to in ((0, own - 2 * block, above), (1, own + 2 * block, below)):
+            pltpu.make_async_remote_copy(
+                kv.at[h, which, rows_of(own, u), :], kv.at[h, which, rows_of(target, u), :],
+                ring_send.at[h, which, slot], ring_recv.at[h, which, slot],
+                device_id=at_blk(to), device_id_type=MESH,
+            ).start()
+
+    def store_own(unit):
+        h, which = unit
+        kv[h, which, rows_of(own, mine), :] = keys_out[h, mine] if which == 0 else values[:, columns(mine, h)]
+
+    far_source = own + (4 - 8 * core) * block
+    far_target = own + (6 - 12 * core) * block
+    far_to = lax.rem(me + blocks + 4 * core - 2, blocks)
+
+    def piece_start(i):
+        return (LOWER_FIRST[i] + core * (UPPER_FIRST[i] - LOWER_FIRST[i])) * TILE
+
+    def step_own(k):
+        if k >= n_units:
+            return
         h, which = unit = units[k]
-
-        def forward(u):
-            for slot, target, to in ((0, own - 2 * block, above), (1, own + 2 * block, below)):
-                pltpu.make_async_remote_copy(
-                    kv.at[h, which, rows_of(own, u), :], kv.at[h, which, rows_of(target, u), :],
-                    ring_send.at[h, which, slot], ring_recv.at[h, which, slot],
-                    device_id=at_blk(to), device_id_type=MESH,
-                ).start()
 
         def one(d, carry):
             u = lax.rem(mine + peers - d, peers)
-            wait_bytes(kv.at[h, which, rows_of(own, u), :], early_recv.at[k, d])
-            forward(u)
-            return carry
-
-        forward(mine)
+            wait_bytes(kv.at[h, which, rows_of(own, u), :], piece_recv.at[h, which, d])
+            forward(unit, u)
+            return carry
+
         lax.fori_loop(1, peers, one, 0)
         for slot, target, to in ((0, own - 2 * block, above), (1, own + 2 * block, below)):
             ringed[k, slot] = pltpu.make_async_remote_copy(
@@ -176,23 +179,6 @@
             )
             sent.append(ringed[k, slot])
         shared[k, 0] = share(unit, 0, own)
-
-    far_source = own + (4 - 8 * core) * block
-    far_target = own + (6 - 12 * core) * block
-    far_to = lax.rem(me + blocks + 4 * core - 2, blocks)
-
-    def piece_start(i):
-        return (LOWER_FIRST[i] + core * (UPPER_FIRST[i] - LOWER_FIRST[i])) * TILE
-
-    def step_own(k):
-        if k < EARLY:
-            own_in_pieces(k)
-        elif k < n_units:
-            unit = units[k]
-            wait_spread(unit[1], unit[0])
-            ringed[k, 0] = ring(unit, 0, own, own - 2 * block, block, above)
-            ringed[k, 1] = ring(unit, 1, own, own + 2 * block, block, below)
-            shared[k, 0] = share(unit, 0, own)
 
     def step_next(n):
         if not 0 <= n < n_units:
@@ -310,7 +296,7 @@
         lax.fori_loop(begin, tiles // GROUP if end is None else end, group, 0, unroll=2)
 
     def near_part(h):
-        wait_spread(2, h)
+        wait_bytes(queries_in.at[h, pl.ds(0, rest), :], uly_recv.at[h])
         for which in (1, 0):
             n = units.index((h, which))
             for slot in (0, 1, 2):
@@ -354,18 +340,30 @@
 
     loads[0].wait()
     norm(0, 0)
+    store_own((0, 0))
     loads[1].wait()
+    store_own((0, 1))
     pl.semaphore_wait(barrier, 3 + peers - 1)
+    forward((0, 1), mine)
     spread(1, 0)
+    forward((0, 0), mine)
     spread(0, 0)
+    for h in range(1, heads):
+        store_own((h, 1))
+        forward((h, 1), mine)
     step_own(0)
     norm(0, 1)
+    store_own((1, 0))
+    forward((1, 0), mine)
     spread(1, 1)
     spread(0, 1)
     step_own(1)
-    norm(0, 2)
-    spread(1, 2)
-    spread(0, 2)
+    for h in range(2, heads):
+        norm(0, h)
+        store_own((h, 0))
+        forward((h, 0), mine)
+        spread(1, h)
+        spread(0, h)
     step_next(0)
     loads[2].wait()
     for h in range(heads):
@@ -450,7 +448,7 @@
                 pltpu.VMEM((heads, block, hd), jnp.float32),
                 pltpu.VMEM((tiles, 16, SPAN), jnp.float32),
                 pltpu.VMEM((heads, block, hd), jnp.bfloat16),
-                dma((3,)), dma((3, heads)), dma((3, heads)), dma((EARLY, peers)),
+                dma((3,)), dma((3, heads)), dma((heads,)), dma((heads, 2, peers)),
                 dma((heads, 2, 6)), dma((heads, 2, 6)),
                 dma((heads, 2, 6)), dma((heads, 2, 6)),
                 dma((len(PIECES),)), dma((len(PIECES),)), dma((len(PIECES),)), dma((len(PIECES),)),

time: 111 us -> 109 us (0.982)
  Pallas kernels: 108 us -> 106 us
    pallas_call x1, Pallas kernels: 108 us -> 106 us  [per_device(): pl.pallas_call(functools.partial(kernel, blocks, peers, heads), out_shape...]
where the time goes in v3:
time: 109 us; the launch traced here: 108 us
  Pallas kernels  106 us (97%)
  local copies, waits for them, and re-layouts  2.06 us (2%)
    pallas_call x1, Pallas kernels, per_device(): pl.pallas_call(functools.partial(kernel, blocks, peers, heads), out_shape...  106 us

profile of v3, /device:TPU:1, one launch (start us, length us, event | category | flops | bytes accessed | tf_op | source)
XLA Modules:
  0.0 108.2 jit_solution(7270813758054859599)
XLA Ops:
  0.0 106.1 %shard_map.73 = bf16[128,3072]{1,0:T(8,128)(2,1)} custom-call(s32[16,27]{1,0:T(8,128)} %neighbors.1, s32[1,16]{1,0:T(1,128)} %bitcast.3, bf16[128,3072]{1,0:T(8,128)(2,1)} %queries_hbm.1, bf16[128,3072]{1,0:T(8,128)(2,1)} %keys_hbm.1, bf16[128,3072]{1,0:T(8,128)(2,1)} %values_hbm.1, f32[1,128]{1,0:T(1,128)} %bitcast.4, f32[1,128]{1,0:T(1,128)} %bitcast.5), custom_call_target="tpu_custom_call" | custom-call | tf_op jit(solution)/shard_map/pallas_call | solution.py:434
  106.1 2.1 %copy.9 = bf16[128,3072]{1,0:T(8,128)(2,1)} copy(bf16[128,3072]{1,0:T(8,128)(2,1)} %shard_map.73) | data formatting | bytes 1572864

commit v4 on v3

v4 whole, which is shorter than its diff:
```python
import functools
import math

import jax
import jax.numpy as jnp
from jax import lax
from jax.experimental import pallas as pl
from jax.experimental.pallas import tpu as pltpu
from jax.sharding import PartitionSpec as P

MESH = pl.DeviceIdType.MESH
TILE = 64
WIDE = 20
FRAME = 60
REACH = 6
GROUP = 2
SPAN = (GROUP + 2) * TILE
NEAR = (-WIDE, 0, WIDE)
AHEAD = (FRAME - WIDE, FRAME, FRAME + WIDE)
PARTS = 4
ROWS = GROUP * TILE


def kernel(
    blocks, peers, heads,
    counts, neighbors, queries_hbm, keys_hbm, values_hbm, query_gain, key_gain,
    out,
    queries, keys, values, kv, queries_in, keys_out, queries_out, total, acc, mask, mixed,
    lists, guest_lists, guests, guest_mixed, guest_total, returned, returned_total,
    load_sem, uly_send, uly_recv, piece_recv, ring_send, ring_recv, pair_send, pair_recv,
    push_send, push_recv, list_sem, return_send, return_recv, total_send, total_recv, back_send, back_recv, own_sem,
):
    tokens = queries.shape[0]
    hd = query_gain.shape[1]
    block = tokens * peers
    tiles = block // TILE
    cfg, me, mine = lax.axis_index("cfg"), lax.axis_index("blk"), lax.axis_index("uly")
    core = lax.rem(me, 2)
    above, below = lax.rem(me + 2, blocks), lax.rem(me + blocks - 2, blocks)
    sibling = me + 1 - 2 * core
    upper = lax.rem(me // 2, 2)
    side = 2 * upper - 1
    partner_blk = me - 2 * side
    outer = lax.rem(me + blocks + 2 * side, blocks)
    gets_far = core + upper == 1
    scale = hd ** -0.5 * math.log2(math.e)
    own = REACH * block
    units = [(h, which) for h in range(heads) for which in (1, 0)]
    n_units = len(units)

    def slot_row(step):
        return pl.multiple_of(own + step * block, block)

    @pl.when(gets_far)
    def _():
        for h, which in units:
            kv[h, which, pl.ds(slot_row(6 * side), TILE), :] = jnp.zeros((TILE, hd), jnp.bfloat16)

    @pl.when(jnp.logical_not(gets_far))
    def _():
        for h, which in units:
            kv[h, which, pl.ds(slot_row(5 * side), block // 2), :] = jnp.zeros((block // 2, hd), jnp.bfloat16)

    def at_blk(b):
        return (cfg, b, mine)

    def at_uly(u):
        return (cfg, me, u)

    def partner(d):
        return lax.rem(mine + d, peers)

    barrier = pltpu.get_barrier_semaphore()
    for d in range(1, peers):
        pl.semaphore_signal(barrier, inc=1, device_id=at_uly(partner(d)), device_id_type=MESH)
    for b in (above, below, sibling):
        pl.semaphore_signal(barrier, inc=1, device_id=at_blk(b), device_id_type=MESH)

    loads = [
        pltpu.make_async_copy(source, target, load_sem.at[i])
        for i, (source, target) in enumerate(((keys_hbm, keys), (values_hbm, values), (queries_hbm, queries)))
    ]
    for load in loads:
        load.start()

    def columns(u, h):
        return pl.ds(pl.multiple_of((u * heads + h) * hd, hd), hd)

    def rows_of(start, u):
        return pl.ds(pl.multiple_of(start + u * tokens, tokens), tokens)

    def normed(states, gain, u, h):
        wide = states[:, columns(u, h)].astype(jnp.float32)
        factor = lax.rsqrt(jnp.mean(wide * wide, axis=-1, keepdims=True) + 1e-06)
        return (wide * factor * gain[...]).astype(jnp.bfloat16)

    def norm(kind, h):
        states, gain, target = (queries, query_gain, queries_out) if kind == 2 else (keys, key_gain, keys_out)

        def one(u, carry):
            target[h, u] = normed(states, gain, u, h)
            return carry

        lax.fori_loop(0, peers, one, 0)

    def spread(kind, h):
        if kind == 2:
            landing = queries_in.at[h, rows_of(0, mine), :]
            queries_in[h, rows_of(0, mine), :] = queries_out[h, mine]
        else:
            landing = kv.at[h, kind, rows_of(own, mine), :]

        def send(d, carry):
            u = partner(d)
            if kind == 2:
                source = queries_out.at[h, u]
            elif kind == 1:
                source = values.at[:, columns(u, h)]
            else:
                source = keys_out.at[h, u]
            arrival = uly_recv.at[h] if kind == 2 else piece_recv.at[h, kind, d]
            pltpu.make_async_remote_copy(
                source, landing, uly_send.at[kind, h], arrival, device_id=at_uly(u), device_id_type=MESH,
            ).start()
            return carry

        lax.fori_loop(1, peers, send, 0)

    rest = (peers - 1) * tokens

    def wait_bytes(ref, sem):
        pltpu.make_async_copy(ref, ref, sem).wait()

    sent = []

    def copy_to(source, target, send, recv, b):
        copy = pltpu.make_async_remote_copy(
            source, target, send, recv, device_id=at_blk(b), device_id_type=MESH
        )
        copy.start()
        sent.append(copy)
        return copy

    def block_of(unit, step):
        return kv.at[(*unit, pl.ds(slot_row(step), block), slice(None))]

    def ring(unit, slot, source, target, to):
        return copy_to(
            block_of(unit, source), block_of(unit, target), ring_send.at[(*unit, slot)], ring_recv.at[(*unit, slot)], to
        )

    def share(unit, slot, step):
        return copy_to(
            block_of(unit, step), block_of(unit, step + 2 * core - 1),
            pair_send.at[(*unit, slot)], pair_recv.at[(*unit, slot)], sibling,
        )

    def far_rows(unit, step, many):
        if many:
            return kv.at[(*unit, pl.ds(pl.multiple_of(slot_row(step) + block // 2, block // 2), block // 2), slice(None))]
        start = pl.multiple_of(slot_row(step) + (1 - core) * (block - TILE), TILE)
        return kv.at[(*unit, pl.ds(start, TILE), slice(None))]

    def far_copy(unit, slot, source, target, to, many):
        for flag, half in ((many, True), (jnp.logical_not(many), False)):

            @pl.when(flag)
            def _():
                pltpu.make_async_remote_copy(
                    far_rows(unit, source, half), far_rows(unit, target, half),
                    ring_send.at[(*unit, slot)], ring_recv.at[(*unit, slot)],
                    device_id=at_blk(to), device_id_type=MESH,
                ).start()

    def far_wait(unit, sem, many):
        for flag, rows in ((many, block // 2), (jnp.logical_not(many), TILE)):

            @pl.when(flag)
            def _():
                wait_bytes(kv.at[(*unit, pl.ds(own, rows), slice(None))], sem)

    ringed, shared = {}, {}

    def forward(unit, u):
        h, which = unit
        for slot, target, to in ((0, own - 2 * block, above), (1, own + 2 * block, below)):
            pltpu.make_async_remote_copy(
                kv.at[h, which, rows_of(own, u), :], kv.at[h, which, rows_of(target, u), :],
                ring_send.at[h, which, slot], ring_recv.at[h, which, slot],
                device_id=at_blk(to), device_id_type=MESH,
            ).start()

    def store_own(unit):
        h, which = unit
        kv[h, which, rows_of(own, mine), :] = keys_out[h, mine] if which == 0 else values[:, columns(mine, h)]

    def step_own(k):
        if k >= n_units:
            return
        h, which = unit = units[k]

        def one(d, carry):
            u = lax.rem(mine + peers - d, peers)
            wait_bytes(kv.at[h, which, rows_of(own, u), :], piece_recv.at[h, which, d])
            forward(unit, u)
            return carry

        lax.fori_loop(1, peers, one, 0)
        for slot, target, to in ((0, -2, above), (1, 2, below)):
            ringed[k, slot] = pltpu.make_async_remote_copy(
                block_of(unit, 0), block_of(unit, target), ring_send.at[h, which, slot], ring_recv.at[h, which, slot],
                device_id=at_blk(to), device_id_type=MESH,
            )
            sent.append(ringed[k, slot])
        shared[k, 0] = share(unit, 0, 0)

    def step_next(n):
        unit = units[n]
        ringed[n, 0].wait_recv()
        ringed[n, 1].wait_recv()
        ringed[n, 2] = ring(unit, 2, -2 * side, -4 * side, outer)
        far_copy(unit, 3, 2 * side, 4 * side, partner_blk, gets_far)
        shared[n, 1] = share(unit, 1, -2)
        shared[n, 2] = share(unit, 2, 2)

    def step_second(n):
        ringed[n, 2].wait_recv()
        shared[n, 3] = share(units[n], 3, 4 * side)

    def step_far(n):
        unit = units[n]
        far_wait(unit, ring_recv.at[(*unit, 3)], jnp.logical_not(gets_far))
        far_copy(unit, 4, -4 * side, -6 * side, outer, jnp.logical_not(gets_far))

    def far_share(n):
        unit = units[n]
        far_wait(unit, ring_recv.at[(*unit, 4)], gets_far)

        @pl.when(gets_far)
        def _():
            pltpu.make_async_remote_copy(
                far_rows(unit, 6 * side, True), far_rows(unit, 6 * side + 2 * core - 1, True),
                pair_send.at[(*unit, 4)], pair_recv.at[(*unit, 4)], device_id=at_blk(sibling), device_id_type=MESH,
            ).start()

    def far_share_wait(n):
        unit = units[n]

        @pl.when(jnp.logical_not(gets_far))
        def _():
            wait_bytes(far_rows(unit, 0, True), pair_recv.at[(*unit, 4)])

    def push(h):
        wait_bytes(queries_in.at[h, pl.ds(0, rest), :], uly_recv.at[h])
        pushed[h] = copy_to(queries_in.at[h], guests.at[h], push_send.at[h], push_recv.at[h], partner_blk)

    pushed = {}

    def list_tiles():
        shape = neighbors.shape
        row = lax.broadcasted_iota(jnp.int32, shape, 0)
        count = jnp.zeros(shape, jnp.int32)
        for t in range(tiles):
            count = jnp.where(row == t, counts[0, t], count)
        live = lax.broadcasted_iota(jnp.int32, shape, 1) < count
        lists[...] = jnp.full(lists.shape, -(2 ** 20), jnp.int32)
        lists[:, : shape[1]] = jnp.where(live, neighbors[...], -(2 ** 20))

    def build_mask(first, centres, entries, blk):
        shape = (tiles, SPAN)
        row = lax.broadcasted_iota(jnp.int32, shape, 0)
        place = lax.broadcasted_iota(jnp.int32, shape, 1) // TILE
        base = blk * tiles + row - 1 - lax.rem(row, GROUP) + place
        listed = entries[...]
        for i, centre in enumerate(centres):
            live = jnp.zeros(shape, jnp.float32)
            for n in range(neighbors.shape[1]):
                live = jnp.where(base + centre == listed[:, n : n + 1], 1.0, live)
            for t in range(tiles):
                mask[t, first + i : first + i + 1, :] = live[t : t + 1, :]

    def windows_sum(h, t, q, windows, sums, result):
        def near(centre):
            return pl.ds(pl.multiple_of(own + (t + centre - 1) * TILE, TILE), SPAN)

        def score(centre):
            return lax.dot_general(
                q, kv[h, 0, near(centre), :], (((1,), (1,)), ((), ())), preferred_element_type=jnp.float32
            )

        scores = score(windows[0][0])
        for i, (centre, line) in enumerate(windows):
            coming = score(windows[i + 1][0]) if i + 1 < len(windows) else None
            live = jnp.concatenate(
                [jnp.broadcast_to(mask[t + a, line : line + 1, :], (TILE, SPAN)) for a in range(GROUP)], axis=0
            )
            weights = jnp.exp2(scores * scale) * live
            for part in range(0, SPAN, 128):
                sums = sums + weights[:, part : part + 128]
            result = result + jnp.dot(
                weights.astype(jnp.bfloat16), kv[h, 1, near(centre), :], preferred_element_type=jnp.float32
            )
            scores = coming
        return sums, result

    def over_groups(work, begin=0, end=PARTS):
        each = tiles // GROUP // PARTS

        def part(i, carry):
            for s in range(each):
                t = (i * each + s) * GROUP
                work(i, s, t, pl.ds(pl.multiple_of(t * TILE, ROWS), ROWS))
            return carry

        lax.fori_loop(begin, end, part, 0)

    zeros = functools.partial(jnp.zeros, dtype=jnp.float32)

    def home(h):
        for which in (1, 0):
            for slot in (0, 1, 2):
                shared[units.index((h, which)), slot].wait_recv()

        def work(i, s, t, rows):
            windows = [(centre, line) for line, centre in enumerate(NEAR)]
            total[h, rows, :], acc[h, rows, :] = windows_sum(
                h, t, queries_in[h, rows, :], windows, zeros((ROWS, 128)), zeros((ROWS, hd))
            )

        over_groups(work)

    def diagonal():
        return lax.broadcasted_iota(jnp.int32, (ROWS, 128), 0) == lax.broadcasted_iota(jnp.int32, (ROWS, 128), 1)

    return_copies = {}

    def guest(h):
        for which in (1, 0):
            shared[units.index((h, which)), 3].wait_recv()
        pushed[h].wait_recv()

        def work(i, s, t, rows):
            windows = [(side * (ahead - 2 * tiles), 6 + j) for j, ahead in enumerate(AHEAD)]
            sums, result = windows_sum(h, t, guests[h, rows, :], windows, zeros((ROWS, 128)), zeros((ROWS, hd)))
            guest_mixed[h, rows, :] = result.astype(jnp.bfloat16)
            column = jnp.sum(sums, axis=-1, keepdims=True)
            guest_total[h, i, s : s + 1, :] = jnp.sum(jnp.where(diagonal(), column, 0.0), axis=0, keepdims=True)

        for i in range(PARTS):
            over_groups(work, i, i + 1)
            rows = pl.ds(i * (block // PARTS), block // PARTS)
            return_copies[h, i, 0] = copy_to(
                guest_mixed.at[h, rows, :], returned.at[h, rows, :], return_send.at[h, i], return_recv.at[h, i], partner_blk
            )
            return_copies[h, i, 1] = copy_to(
                guest_total.at[h, i], returned_total.at[h, i], total_send.at[h, i], total_recv.at[h, i], partner_blk
            )

    def middle(h):
        def work(i, s, t, rows):
            windows = [(side * ahead, 3 + j) for j, ahead in enumerate(AHEAD[:2])]
            total[h, rows, :], acc[h, rows, :] = windows_sum(
                h, t, queries_in[h, rows, :], windows, total[h, rows, :], acc[h, rows, :]
            )

        over_groups(work)

    def finish(h):
        for which in (1, 0):
            far_share_wait(units.index((h, which)))

        def work(i, s, t, rows):
            sums, result = windows_sum(
                h, t, queries_in[h, rows, :], [(side * AHEAD[2], 5)], total[h, rows, :], acc[h, rows, :]
            )
            line = returned_total[h, i, s : s + 1, :]
            sums = sums + jnp.where(diagonal(), jnp.broadcast_to(line, (ROWS, 128)), 0.0)
            result = result + returned[h, rows, :].astype(jnp.float32)
            mixed[h, rows, :] = (result / jnp.sum(sums, axis=-1, keepdims=True)).astype(jnp.bfloat16)

        each = peers // PARTS
        for i in range(PARTS):
            return_copies[h, i, 0].wait_recv()
            return_copies[h, i, 1].wait_recv()
            over_groups(work, i, i + 1)
            for u in range(i * each, (i + 1) * each):
                send_back(h, u)

    def send_back(h, u):
        source = mixed.at[h, rows_of(0, u), :]
        landing = out.at[:, columns(mine, h)]

        @pl.when(u != mine)
        def _():
            pltpu.make_async_remote_copy(
                source, landing, back_send.at[h], back_recv.at[h], device_id=at_uly(u), device_id_type=MESH,
            ).start()

        @pl.when(u == mine)
        def _():
            pltpu.make_async_copy(source, landing, own_sem.at[h]).start()

    loads[0].wait()
    norm(0, 0)
    store_own((0, 0))
    loads[1].wait()
    store_own((0, 1))
    pl.semaphore_wait(barrier, 3 + peers - 1)
    forward((0, 1), mine)
    spread(1, 0)
    forward((0, 0), mine)
    spread(0, 0)
    for h in range(1, heads):
        store_own((h, 1))
        forward((h, 1), mine)
    step_own(0)
    norm(0, 1)
    store_own((1, 0))
    forward((1, 0), mine)
    spread(1, 1)
    spread(0, 1)
    step_own(1)
    loads[2].wait()
    norm(2, 0)
    spread(2, 0)
    for h in range(2, heads):
        norm(0, h)
        store_own((h, 0))
        forward((h, 0), mine)
        spread(1, h)
        spread(0, h)
    step_next(0)
    for h in range(1, heads):
        norm(2, h)
        spread(2, h)
    list_tiles()
    lists_copy = copy_to(lists, guest_lists, list_sem.at[0], list_sem.at[1], partner_blk)
    guest_total[...] = jnp.zeros(guest_total.shape, jnp.float32)
    step_own(2)
    push(0)
    step_next(1)
    step_second(0)
    build_mask(0, NEAR, lists, me)
    step_own(3)
    step_next(2)
    step_second(1)
    push(1)
    home(0)
    build_mask(3, [side * ahead for ahead in AHEAD], lists, me)
    lists_copy.wait_recv()
    build_mask(6, [side * ahead for ahead in AHEAD], guest_lists, partner_blk)
    step_own(4)
    step_next(3)
    step_second(2)
    push(2)
    guest(0)
    middle(0)
    step_own(5)
    step_next(4)
    step_second(3)
    home(1)
    step_next(5)
    for n in range(n_units - 1):
        step_far(n)
    step_second(4)
    guest(1)
    middle(1)
    home(2)
    step_far(n_units - 1)
    step_second(5)
    guest(2)
    for h in range(heads):
        far_share(2 * h)
        far_share(2 * h + 1)
        if h == heads - 1:
            middle(h)
        finish(h)

    for copy in sent:
        copy.wait_send()
    for unit in units:
        far_wait(unit, ring_send.at[(*unit, 3)], gets_far)
        far_wait(unit, ring_send.at[(*unit, 4)], jnp.logical_not(gets_far))

        @pl.when(gets_far)
        def _():
            wait_bytes(far_rows(unit, 0, True), pair_send.at[(*unit, 4)])

    for h in range(heads):
        for kind in range(3):
            wait_bytes(queries_in.at[h, pl.ds(0, rest), :], uly_send.at[kind, h])
        wait_bytes(queries_in.at[h, pl.ds(0, rest), :], back_send.at[h])
        wait_bytes(queries_in.at[h, pl.ds(0, tokens), :], own_sem.at[h])
    for h in range(heads):
        wait_bytes(queries_in.at[h, pl.ds(0, rest), :], back_recv.at[h])


def solution(mesh):
    blocks, peers = mesh.shape["blk"], mesh.shape["uly"]

    def per_device(queries, keys, values, query_gain, key_gain, neighbors, counts):
        tokens, width = queries.shape
        hd = query_gain.shape[0]
        heads = width // hd // peers
        block = tokens * peers
        tiles = block // TILE
        vmem = pl.BlockSpec(memory_space=pltpu.VMEM)
        smem = pl.BlockSpec(memory_space=pltpu.SMEM)
        dma = pltpu.SemaphoreType.DMA
        return pl.pallas_call(
            functools.partial(kernel, blocks, peers, heads),
            out_shape=jax.ShapeDtypeStruct((tokens, width), jnp.bfloat16),
            in_specs=[smem, vmem] + [pl.BlockSpec(memory_space=pl.ANY)] * 3 + [vmem] * 2,
            out_specs=pl.BlockSpec(memory_space=pl.ANY),
            scratch_shapes=[
                pltpu.VMEM((tokens, width), jnp.bfloat16),
                pltpu.VMEM((tokens, width), jnp.bfloat16),
                pltpu.VMEM((tokens, width), jnp.bfloat16),
                pltpu.VMEM((heads, 2, (2 * REACH + 1) * block, hd), jnp.bfloat16),
                pltpu.VMEM((heads, block, hd), jnp.bfloat16),
                pltpu.VMEM((heads, peers, tokens, hd), jnp.bfloat16),
                pltpu.VMEM((heads, peers, tokens, hd), jnp.bfloat16),
                pltpu.VMEM((heads, block, 128), jnp.float32),
                pltpu.VMEM((heads, block, hd), jnp.float32),
                pltpu.VMEM((tiles, 16, SPAN), jnp.float32),
                pltpu.VMEM((heads, block, hd), jnp.bfloat16),
                pltpu.VMEM((tiles, 128), jnp.int32),
                pltpu.VMEM((tiles, 128), jnp.int32),
                pltpu.VMEM((heads, block, hd), jnp.bfloat16),
                pltpu.VMEM((heads, block, hd), jnp.bfloat16),
                pltpu.VMEM((heads, PARTS, 8, 128), jnp.float32),
                pltpu.VMEM((heads, block, hd), jnp.bfloat16),
                pltpu.VMEM((heads, PARTS, 8, 128), jnp.float32),
                dma((3,)), dma((3, heads)), dma((heads,)), dma((heads, 2, peers)),
                dma((heads, 2, 5)), dma((heads, 2, 5)),
                dma((heads, 2, 5)), dma((heads, 2, 5)),
                dma((heads,)), dma((heads,)), dma((2,)),
                dma((heads, PARTS)), dma((heads, PARTS)), dma((heads, PARTS)), dma((heads, PARTS)),
                dma((heads,)), dma((heads,)), dma((heads,)),
            ],
            compiler_params=pltpu.CompilerParams(
                collective_id=0, has_side_effects=True, vmem_limit_bytes=56 * 2 ** 20
            ),
        )(counts.reshape(1, -1), neighbors, queries, keys, values, query_gain.reshape(1, -1), key_gain.reshape(1, -1))

    tokens = P(("cfg", "blk", "uly"), None)
    return jax.shard_map(
        per_device,
        mesh=mesh,
        in_specs=(tokens, tokens, tokens, P(), P(), P("blk", None), P("blk")),
        out_specs=tokens,
        check_vma=False,
    )
```

time: 109 us -> 105 us (0.963)
  Pallas kernels: 106 us -> 103 us
    pallas_call x1, Pallas kernels: 106 us -> 103 us  [per_device(): pl.pallas_call(functools.partial(kernel, blocks, peers, heads), out_shape...]
where the time goes in v4:
time: 105 us
  Pallas kernels  103 us (98%)
  local copies, waits for them, and re-layouts  2.06 us (2%)
    pallas_call x1, Pallas kernels, per_device(): pl.pallas_call(functools.partial(kernel, blocks, peers, heads), out_shape...  103 us

profile of v4, /device:TPU:1, one launch (start us, length us, event | category | flops | bytes accessed | tf_op | source)
XLA Modules:
  0.0 104.8 jit_solution(6079015199791929769)
XLA Ops:
  0.0 102.7 %shard_map.73 = bf16[128,3072]{1,0:T(8,128)(2,1)} custom-call(s32[1,16]{1,0:T(1,128)} %bitcast.3, s32[16,27]{1,0:T(8,128)} %neighbors.1, bf16[128,3072]{1,0:T(8,128)(2,1)} %queries_hbm.1, bf16[128,3072]{1,0:T(8,128)(2,1)} %keys_hbm.1, bf16[128,3072]{1,0:T(8,128)(2,1)} %values_hbm.1, f32[1,128]{1,0:T(1,128)} %bitcast.4, f32[1,128]{1,0:T(1,128)} %bitcast.5), custom_call_target="tpu_custom_call" | custom-call | tf_op jit(solution)/shard_map/pallas_call | solution.py:510
  102.7 2.1 %copy.9 = bf16[128,3072]{1,0:T(8,128)(2,1)} copy(bf16[128,3072]{1,0:T(8,128)(2,1)} %shard_map.73) | data formatting | bytes 1572864

commit v5 on v4

--- a/solution.py
+++ b/solution.py
@@ -42,7 +42,12 @@
     side = 2 * upper - 1
     partner_blk = me - 2 * side
     outer = lax.rem(me + blocks + 2 * side, blocks)
-    gets_far = core + upper == 1
+    outer_sibling = outer + 1 - 2 * core
+    gets_half = core == upper
+    gives_half = core + upper == 1
+    gives_one = core + upper == 2
+    gets_one = core - upper == 1
+    is_one = core == 1
     scale = hd ** -0.5 * math.log2(math.e)
     own = REACH * block
     units = [(h, which) for h in range(heads) for which in (1, 0)]
@@ -51,16 +56,6 @@
     def slot_row(step):
         return pl.multiple_of(own + step * block, block)
 
-    @pl.when(gets_far)
-    def _():
-        for h, which in units:
-            kv[h, which, pl.ds(slot_row(6 * side), TILE), :] = jnp.zeros((TILE, hd), jnp.bfloat16)
-
-    @pl.when(jnp.logical_not(gets_far))
-    def _():
-        for h, which in units:
-            kv[h, which, pl.ds(slot_row(5 * side), block // 2), :] = jnp.zeros((block // 2, hd), jnp.bfloat16)
-
     def at_blk(b):
         return (cfg, b, mine)
 
@@ -73,7 +68,7 @@
     barrier = pltpu.get_barrier_semaphore()
     for d in range(1, peers):
         pl.semaphore_signal(barrier, inc=1, device_id=at_uly(partner(d)), device_id_type=MESH)
-    for b in (above, below, sibling):
+    for b in (above, below, sibling, outer_sibling):
         pl.semaphore_signal(barrier, inc=1, device_id=at_blk(b), device_id_type=MESH)
 
     loads = [
@@ -82,6 +77,17 @@
     ]
     for load in loads:
         load.start()
+
+    @pl.when(core == 0)
+    def _():
+        start = pl.multiple_of(own - 5 * block - TILE + upper * (11 * block + TILE), TILE)
+        for h, which in units:
+            kv[h, which, pl.ds(start, TILE), :] = jnp.zeros((TILE, hd), jnp.bfloat16)
+
+    @pl.when(gets_half)
+    def _():
+        for h, which in units:
+            kv[h, which, pl.ds(slot_row(5 * side), block // 2), :] = jnp.zeros((block // 2, hd), jnp.bfloat16)
 
     def columns(u, h):
         return pl.ds(pl.multiple_of((u * heads + h) * hd, hd), hd)
@@ -155,29 +161,24 @@
             pair_send.at[(*unit, slot)], pair_recv.at[(*unit, slot)], sibling,
         )
 
-    def far_rows(unit, step, many):
-        if many:
-            return kv.at[(*unit, pl.ds(pl.multiple_of(slot_row(step) + block // 2, block // 2), block // 2), slice(None))]
-        start = pl.multiple_of(slot_row(step) + (1 - core) * (block - TILE), TILE)
-        return kv.at[(*unit, pl.ds(start, TILE), slice(None))]
-
-    def far_copy(unit, slot, source, target, to, many):
-        for flag, half in ((many, True), (jnp.logical_not(many), False)):
-
-            @pl.when(flag)
-            def _():
-                pltpu.make_async_remote_copy(
-                    far_rows(unit, source, half), far_rows(unit, target, half),
-                    ring_send.at[(*unit, slot)], ring_recv.at[(*unit, slot)],
-                    device_id=at_blk(to), device_id_type=MESH,
-                ).start()
-
-    def far_wait(unit, sem, many):
-        for flag, rows in ((many, block // 2), (jnp.logical_not(many), TILE)):
-
-            @pl.when(flag)
-            def _():
-                wait_bytes(kv.at[(*unit, pl.ds(own, rows), slice(None))], sem)
+    def half_of(unit, step):
+        return kv.at[(*unit, pl.ds(pl.multiple_of(slot_row(step) + block // 2, block // 2), block // 2), slice(None))]
+
+    def tile_of(unit, step, tile):
+        return kv.at[(*unit, pl.ds(pl.multiple_of(slot_row(step) + tile * TILE, TILE), TILE), slice(None))]
+
+    def copy_if(flag, unit, slot, source, target, to):
+        @pl.when(flag)
+        def _():
+            pltpu.make_async_remote_copy(
+                source, target, ring_send.at[(*unit, slot)], ring_recv.at[(*unit, slot)],
+                device_id=at_blk(to), device_id_type=MESH,
+            ).start()
+
+    def wait_if(flag, sem, rows):
+        @pl.when(flag)
+        def _():
+            wait_bytes(kv.at[0, 0, pl.ds(own, rows), :], sem)
 
     ringed, shared = {}, {}
 
@@ -219,7 +220,8 @@
         ringed[n, 0].wait_recv()
         ringed[n, 1].wait_recv()
         ringed[n, 2] = ring(unit, 2, -2 * side, -4 * side, outer)
-        far_copy(unit, 3, 2 * side, 4 * side, partner_blk, gets_far)
+        copy_if(gives_half, unit, 3, half_of(unit, 2 * side), half_of(unit, 4 * side), partner_blk)
+        copy_if(gives_one, unit, 3, tile_of(unit, 2, 0), tile_of(unit, 4, 0), partner_blk)
         shared[n, 1] = share(unit, 1, -2)
         shared[n, 2] = share(unit, 2, 2)
 
@@ -229,26 +231,13 @@
 
     def step_far(n):
         unit = units[n]
-        far_wait(unit, ring_recv.at[(*unit, 3)], jnp.logical_not(gets_far))
-        far_copy(unit, 4, -4 * side, -6 * side, outer, jnp.logical_not(gets_far))
-
-    def far_share(n):
-        unit = units[n]
-        far_wait(unit, ring_recv.at[(*unit, 4)], gets_far)
-
-        @pl.when(gets_far)
-        def _():
-            pltpu.make_async_remote_copy(
-                far_rows(unit, 6 * side, True), far_rows(unit, 6 * side + 2 * core - 1, True),
-                pair_send.at[(*unit, 4)], pair_recv.at[(*unit, 4)], device_id=at_blk(sibling), device_id_type=MESH,
-            ).start()
-
-    def far_share_wait(n):
-        unit = units[n]
-
-        @pl.when(jnp.logical_not(gets_far))
-        def _():
-            wait_bytes(far_rows(unit, 0, True), pair_recv.at[(*unit, 4)])
+        last_tile = upper * (tiles - 1)
+        wait_if(gets_half, ring_recv.at[(*unit, 3)], block // 2)
+        wait_if(gets_one, ring_recv.at[(*unit, 3)], TILE)
+        copy_if(
+            gets_half, unit, 4, half_of(unit, -4 * side), half_of(unit, 2 * core - 1 - 6 * side), outer_sibling
+        )
+        copy_if(is_one, unit, 5, tile_of(unit, -4 * side, last_tile), tile_of(unit, -6 * side, last_tile), outer)
 
     def push(h):
         wait_bytes(queries_in.at[h, pl.ds(0, rest), :], uly_recv.at[h])
@@ -367,7 +356,8 @@
 
     def finish(h):
         for which in (1, 0):
-            far_share_wait(units.index((h, which)))
+            wait_if(gets_half, ring_recv.at[h, which, 4], block // 2)
+            wait_if(is_one, ring_recv.at[h, which, 5], TILE)
 
         def work(i, s, t, rows):
             sums, result = windows_sum(
@@ -405,7 +395,7 @@
     store_own((0, 0))
     loads[1].wait()
     store_own((0, 1))
-    pl.semaphore_wait(barrier, 3 + peers - 1)
+    pl.semaphore_wait(barrier, 4 + peers - 1)
     forward((0, 1), mine)
     spread(1, 0)
     forward((0, 0), mine)
@@ -457,35 +447,33 @@
     middle(0)
     step_own(5)
     step_next(4)
+    step_far(0)
+    step_far(1)
     step_second(3)
     home(1)
     step_next(5)
-    for n in range(n_units - 1):
-        step_far(n)
+    step_far(2)
+    step_far(3)
+    step_far(4)
+    guest(1)
     step_second(4)
-    guest(1)
     middle(1)
+    finish(0)
     home(2)
-    step_far(n_units - 1)
+    step_far(5)
     step_second(5)
     guest(2)
-    for h in range(heads):
-        far_share(2 * h)
-        far_share(2 * h + 1)
-        if h == heads - 1:
-            middle(h)
-        finish(h)
+    finish(1)
+    middle(2)
+    finish(2)
 
     for copy in sent:
         copy.wait_send()
     for unit in units:
-        far_wait(unit, ring_send.at[(*unit, 3)], gets_far)
-        far_wait(unit, ring_send.at[(*unit, 4)], jnp.logical_not(gets_far))
-
-        @pl.when(gets_far)
-        def _():
-            wait_bytes(far_rows(unit, 0, True), pair_send.at[(*unit, 4)])
-
+        wait_if(gives_half, ring_send.at[(*unit, 3)], block // 2)
+        wait_if(gives_one, ring_send.at[(*unit, 3)], TILE)
+        wait_if(gets_half, ring_send.at[(*unit, 4)], block // 2)
+        wait_if(is_one, ring_send.at[(*unit, 5)], TILE)
     for h in range(heads):
         for kind in range(3):
             wait_bytes(queries_in.at[h, pl.ds(0, rest), :], uly_send.at[kind, h])
@@ -532,8 +520,8 @@
                 pltpu.VMEM((heads, block, hd), jnp.bfloat16),
                 pltpu.VMEM((heads, PARTS, 8, 128), jnp.float32),
                 dma((3,)), dma((3, heads)), dma((heads,)), dma((heads, 2, peers)),
-                dma((heads, 2, 5)), dma((heads, 2, 5)),
-                dma((heads, 2, 5)), dma((heads, 2, 5)),
+                dma((heads, 2, 6)), dma((heads, 2, 6)),
+                dma((heads, 2, 4)), dma((heads, 2, 4)),
                 dma((heads,)), dma((heads,)), dma((2,)),
                 dma((heads, PARTS)), dma((heads, PARTS)), dma((heads, PARTS)), dma((heads, PARTS)),
                 dma((heads,)), dma((heads,)), dma((heads,)),

time: 105 us -> 101 us (0.962)
  Pallas kernels: 103 us -> 98.4 us
    pallas_call x1, Pallas kernels: 103 us -> 98.4 us  [per_device(): pl.pallas_call(functools.partial(kernel, blocks, peers, heads), out_shape...]
where the time goes in v5:
time: 101 us
  Pallas kernels  98.4 us (97%)
  local copies, waits for them, and re-layouts  2.06 us (2%)
    pallas_call x1, Pallas kernels, per_device(): pl.pallas_call(functools.partial(kernel, blocks, peers, heads), out_shape...  98.4 us
    unnamed x1, local copies, waits for them, and re-layouts  2.06 us

profile of v5, /device:TPU:1, one launch (start us, length us, event | category | flops | bytes accessed | tf_op | source)
XLA Modules:
  0.0 100.5 jit_solution(14142617255222315666)
XLA Ops:
  0.0 98.4 %shard_map.73 = bf16[128,3072]{1,0:T(8,128)(2,1)} custom-call(s32[1,16]{1,0:T(1,128)} %bitcast.3, s32[16,27]{1,0:T(8,128)} %neighbors.1, bf16[128,3072]{1,0:T(8,128)(2,1)} %queries_hbm.1, bf16[128,3072]{1,0:T(8,128)(2,1)} %keys_hbm.1, bf16[128,3072]{1,0:T(8,128)(2,1)} %values_hbm.1, f32[1,128]{1,0:T(1,128)} %bitcast.4, f32[1,128]{1,0:T(1,128)} %bitcast.5), custom_call_target="tpu_custom_call" | custom-call | tf_op jit(solution)/shard_map/pallas_call | solution.py:498
  98.4 2.1 %copy.9 = bf16[128,3072]{1,0:T(8,128)(2,1)} copy(bf16[128,3072]{1,0:T(8,128)(2,1)} %shard_map.73) | data formatting | bytes 1572864

commit v6 on v5

--- a/solution.py
+++ b/solution.py
@@ -355,9 +355,9 @@
         over_groups(work)
 
     def finish(h):
-        for which in (1, 0):
-            wait_if(gets_half, ring_recv.at[h, which, 4], block // 2)
-            wait_if(is_one, ring_recv.at[h, which, 5], TILE)
+        def wait_far(flag, slot, rows):
+            for which in (1, 0):
+                wait_if(flag, ring_recv.at[h, which, slot], rows)
 
         def work(i, s, t, rows):
             sums, result = windows_sum(
@@ -372,6 +372,12 @@
         for i in range(PARTS):
             return_copies[h, i, 0].wait_recv()
             return_copies[h, i, 1].wait_recv()
+            if i == 0:
+                wait_far(gets_one, 5, TILE)
+            if i == 1:
+                wait_far(gets_half, 4, block // 2)
+            if i == PARTS - 1:
+                wait_far(gives_one, 5, TILE)
             over_groups(work, i, i + 1)
             for u in range(i * each, (i + 1) * each):
                 send_back(h, u)

time: 101 us -> 101 us (level)
  no operation moved by 1% of the time
where the time goes in v6:
time: 101 us
  Pallas kernels  98.4 us (97%)
  local copies, waits for them, and re-layouts  2.06 us (2%)
    pallas_call x1, Pallas kernels, per_device(): pl.pallas_call(functools.partial(kernel, blocks, peers, heads), out_shape...  98.4 us
    unnamed x1, local copies, waits for them, and re-layouts  2.06 us

profile of v6, /device:TPU:1, one launch (start us, length us, event | category | flops | bytes accessed | tf_op | source)
XLA Modules:
  0.0 100.5 jit_solution(11613460034520219414)
XLA Ops:
  0.0 98.4 %shard_map.73 = bf16[128,3072]{1,0:T(8,128)(2,1)} custom-call(s32[1,16]{1,0:T(1,128)} %bitcast.3, s32[16,27]{1,0:T(8,128)} %neighbors.1, bf16[128,3072]{1,0:T(8,128)(2,1)} %queries_hbm.1, bf16[128,3072]{1,0:T(8,128)(2,1)} %keys_hbm.1, bf16[128,3072]{1,0:T(8,128)(2,1)} %values_hbm.1, f32[1,128]{1,0:T(1,128)} %bitcast.4, f32[1,128]{1,0:T(1,128)} %bitcast.5), custom_call_target="tpu_custom_call" | custom-call | tf_op jit(solution)/shard_map/pallas_call | solution.py:504
  98.4 2.1 %copy.9 = bf16[128,3072]{1,0:T(8,128)(2,1)} copy(bf16[128,3072]{1,0:T(8,128)(2,1)} %shard_map.73) | data formatting | bytes 1572864

commit v7 on v6

--- a/solution.py
+++ b/solution.py
@@ -161,6 +161,10 @@
             pair_send.at[(*unit, slot)], pair_recv.at[(*unit, slot)], sibling,
         )
 
+    def part_of(unit, step, i):
+        start = pl.multiple_of(slot_row(step) + i * (block // 2), block // 2)
+        return kv.at[(*unit, pl.ds(start, block // 2), slice(None))]
+
     def half_of(unit, step):
         return kv.at[(*unit, pl.ds(pl.multiple_of(slot_row(step) + block // 2, block // 2), block // 2), slice(None))]
 
@@ -219,15 +223,32 @@
         unit = units[n]
         ringed[n, 0].wait_recv()
         ringed[n, 1].wait_recv()
-        ringed[n, 2] = ring(unit, 2, -2 * side, -4 * side, outer)
+        if n == n_units - 1:
+            for i, slot in enumerate((2, 6)):
+                ringed[n, slot] = copy_to(
+                    part_of(unit, -2 * side, i), part_of(unit, -4 * side, i),
+                    ring_send.at[(*unit, slot)], ring_recv.at[(*unit, slot)], outer,
+                )
+        else:
+            ringed[n, 2] = ring(unit, 2, -2 * side, -4 * side, outer)
         copy_if(gives_half, unit, 3, half_of(unit, 2 * side), half_of(unit, 4 * side), partner_blk)
         copy_if(gives_one, unit, 3, tile_of(unit, 2, 0), tile_of(unit, 4, 0), partner_blk)
         shared[n, 1] = share(unit, 1, -2)
         shared[n, 2] = share(unit, 2, 2)
 
     def step_second(n):
+        unit = units[n]
         ringed[n, 2].wait_recv()
-        shared[n, 3] = share(units[n], 3, 4 * side)
+        if n < n_units - 1:
+            shared[n, 3] = share(unit, 3, 4 * side)
+            return
+        for i, slot in enumerate((3, 4)):
+            if i == 1:
+                ringed[n, 6].wait_recv()
+            shared[n, slot] = copy_to(
+                part_of(unit, 4 * side, i), part_of(unit, 4 * side + 2 * core - 1, i),
+                pair_send.at[(*unit, slot)], pair_recv.at[(*unit, slot)], sibling,
+            )
 
     def step_far(n):
         unit = units[n]
@@ -325,7 +346,9 @@
 
     def guest(h):
         for which in (1, 0):
-            shared[units.index((h, which)), 3].wait_recv()
+            for slot in (3, 4):
+                if (units.index((h, which)), slot) in shared:
+                    shared[units.index((h, which)), slot].wait_recv()
         pushed[h].wait_recv()
 
         def work(i, s, t, rows):
@@ -526,8 +549,8 @@
                 pltpu.VMEM((heads, block, hd), jnp.bfloat16),
                 pltpu.VMEM((heads, PARTS, 8, 128), jnp.float32),
                 dma((3,)), dma((3, heads)), dma((heads,)), dma((heads, 2, peers)),
-                dma((heads, 2, 6)), dma((heads, 2, 6)),
-                dma((heads, 2, 4)), dma((heads, 2, 4)),
+                dma((heads, 2, 7)), dma((heads, 2, 7)),
+                dma((heads, 2, 5)), dma((heads, 2, 5)),
                 dma((heads,)), dma((heads,)), dma((2,)),
                 dma((heads, PARTS)), dma((heads, PARTS)), dma((heads, PARTS)), dma((heads, PARTS)),
                 dma((heads,)), dma((heads,)), dma((heads,)),

time: 101 us -> 101 us (level)
  no operation moved by 1% of the time
where the time goes in v7:
time: 101 us
  Pallas kernels  98.5 us (98%)
  local copies, waits for them, and re-layouts  2.06 us (2%)
    pallas_call x1, Pallas kernels, per_device(): pl.pallas_call(functools.partial(kernel, blocks, peers, heads), out_shape...  98.5 us
    unnamed x1, local copies, waits for them, and re-layouts  2.06 us

profile of v7, /device:TPU:1, one launch (start us, length us, event | category | flops | bytes accessed | tf_op | source)
XLA Modules:
  0.0 100.5 jit_solution(4983436168990953138)
XLA Ops:
  0.0 98.5 %shard_map.73 = bf16[128,3072]{1,0:T(8,128)(2,1)} custom-call(s32[1,16]{1,0:T(1,128)} %bitcast.3, s32[16,27]{1,0:T(8,128)} %neighbors.1, bf16[128,3072]{1,0:T(8,128)(2,1)} %queries_hbm.1, bf16[128,3072]{1,0:T(8,128)(2,1)} %keys_hbm.1, bf16[128,3072]{1,0:T(8,128)(2,1)} %values_hbm.1, f32[1,128]{1,0:T(1,128)} %bitcast.4, f32[1,128]{1,0:T(1,128)} %bitcast.5), custom_call_target="tpu_custom_call" | custom-call | tf_op jit(solution)/shard_map/pallas_call | solution.py:527
  98.5 2.1 %copy.9 = bf16[128,3072]{1,0:T(8,128)(2,1)} copy(bf16[128,3072]{1,0:T(8,128)(2,1)} %shard_map.73) | data formatting | bytes 1572864
